TPU v7x, 256 devices: a whole 4x4x8 slice. The times are simulated.
256 devices in a mesh: occ: 8 (over z), vir: 16 (over x, y), stream: 2 (over core).
Axes of the slice: x: 4, y: 4, z: 8, core: 2. Of those that a mesh axis runs over, the one named last changes fastest.
Arguments:
- doubles: bfloat16 [3072, 32, 1024], P('occ', 'vir'), may hold values from -6 to 6
- integrals: bfloat16 [16, 2, 2, 2, 1024, 1024], P('vir', 'stream'), may hold values from -0.09375 to 0.09375
- tiles: int32 [16, 2, 2], P('vir', 'stream'), may hold values from 0 to 31, as said below
Outputs:
- ladder: bfloat16 [3072, 32, 1024], P('occ', ('vir', 'stream'))
Inputs may be any that keep to these rules, and one draw needn't show every extreme that they name: tiles[j, k, 0] // 2 equals (j - 1) mod 16 and tiles[j, k, 1] // 2 equals (j + 8) mod 16: slot 0 of vir index j uses a tile pair held by the vir index before it, slot 1 one held by the vir index half the axis away; which of its 2 tile pairs is drawn.
All inputs are finite; a program needn't handle non-finite values.
Results may differ from a plain program's by a relative error of at most 0.001.
Values may be sent and summed in bfloat16 or wider, within the bound.
No kernel may reach another device: no remote copies, remote signals or barrier semaphores. Data moves between devices by JAX's collectives and lax.ppermute only.
A program may use at most 128 MiB of HBM per device.

v0:
```python
import jax
import jax.numpy as jnp
from jax import lax
from jax.sharding import PartitionSpec as P


def on_device(doubles, integrals, tiles):
    used = tiles[0, 0]
    whole = lax.all_gather(doubles, "vir", axis=1, tiled=True)
    picked = jnp.take(whole, used, axis=1)
    partial_value = jnp.einsum(
        "osq,aspq->oap", picked, integrals[0, 0], preferred_element_type=jnp.float32
    )
    summed = lax.psum(partial_value, "stream")
    result = lax.dynamic_slice_in_dim(summed, lax.axis_index("stream"), 1, 1)
    return result.astype(jnp.bfloat16)


def solution(mesh):
    placed = (
        P("occ", "vir", None),
        P("vir", "stream", None, None, None, None),
        P("vir", "stream", None),
    )
    return jax.shard_map(
        on_device,
        mesh=mesh,
        in_specs=placed,
        out_specs=P("occ", ("vir", "stream"), None),
        check_vma=False,
    )
```

profile of v0, /device:TPU:1, one launch (start us, length us, event | category | flops | bytes accessed | tf_op | source)
XLA Modules:
  0.0 210.8 jit_solution(9752640016382919560)
XLA Ops:
  6.5 0.0 all-gather.2.cloned.1.call-start
  6.5 3.1 %copy.6 = bf16[384,2,1024]{2,0,1:T(8,128)(2,1)} copy(bf16[384,2,1024]{2,1,0:T(2,128)(2,1)} %param.3) | data formatting | bytes 3145728 | tf_op args[0]
  9.6 0.0 copy-start
  9.6 0.0 all-gather.2.cloned.1.call-update
  9.7 0.6 copy-done
  10.3 162.6 %all-gather.2.cloned.1.call-done = bf16[384,32,1024]{2,0,1:T(8,128)(2,1)} async-done(((bf16[384,2,1024]{2,0,1:T(8,128)(2,1)}), bf16[384,32,1024]{2,0,1:T(8,128)(2,1)}) %all-gather.2.cloned.1.call-update) | async-done | bytes 25165840 | tf_op jit(solution)/shard_map/all_gather | solution.py:9
  172.9 8.8 %gather_fusion = bf16[2,384,1024]{2,1,0:T(8,128)(2,1)S(1)} fusion(bf16[384,32,1024]{2,0,1:T(8,128)(2,1)} %all-gather.2.cloned.1.call-done, s32[1024]{0:T(1024)S(1)} %pad_clamp_fusion), kind=kCustom, calls=%fused_computation | custom fusion | bytes 3145736 | tf_op jit(solution)/shard_map/jit(_take)/gather | solution.py:10
  181.7 8.5 %fusion.2 = f32[384,2,1024]{2,0,1:T(8,128)} fusion(bf16[1,1,2,2,1024,1024]{5,4,3,2,1,0:T(8,128)(2,1)} %param.4, bf16[2,384,1024]{2,1,0:T(8,128)(2,1)S(1)} %gather_fusion, pred[2]{0:T(512)(128)(4,1)S(1)} %compare_and_fusion), kind=kOutput, calls=%fused_computation.3 | convolution fusion | flops 3222011904 | bytes 13107202 | tf_op jit(solution)/shard_map/osq,aspq->oap/dot_general | solution.py:11
  190.2 12.8 %all-reduce.1 = bf16[384,2,1024]{2,0,1:T(8,128)(2,1)S(1)} all-reduce(f32[384,2,1024]{2,0,1:T(8,128)} %fusion.2), channel_id=1, replica_groups=mesh['occ'=8,'vir'=16,'stream'=2] {'stream'}, use_global_device_ids=true, to_apply=%region_0.1 | all-reduce | flops 786432 | bytes 4718592 | tf_op jit(solution)/shard_map/psum | solution.py:14
  203.0 0.9 dynamic-slice_convert_fusion
  (3 shorter events, 0.0 us)
Async XLA Ops:
  6.5 166.3 %all-gather.2.cloned.1.call-start = ((), (), s32[]{:S(2)}) async-start(), calls=%async_computation | async-start | bytes 26738688 | tf_op jit(solution)/shard_map/all_gather | solution.py:9
  9.6 0.7 copy-start
Sparse Core Ops, SparseCore 0:
  9.8 162.9 all-gather.1
where the time goes:
time: 211 us
  waiting for transfers between devices  163 us (77%)
  local copies, waits for them, and re-layouts  13.5 us (6%)
  between operations  13.4 us (6%)
  blocking collectives  12.8 us (6%)
  matrix products  8.54 us (4%)
    all_gather x1, waiting for transfers between devices, on_device(): whole = lax.all_gather(doubles, 'vir', axis=1, tiled=True)  163 us
    psum x1, blocking collectives, on_device(): summed = lax.psum(partial_value, 'stream')  12.8 us
    gather x1, local copies, waits for them, and re-layouts, on_device(): picked = jnp.take(whole, used, axis=1)  8.8 us
    dot_general x1, matrix products, on_device(): jnp.einsum('osq,aspq->oap', picked, integrals[0, 0], preferred_element_ty...  8.54 us
  transfers between devices with their start and end apart: 1, of which 1 were waited for; matrix products, arithmetic and copies ran while one was open for 0% of the time, Pallas kernels for 0%

commit v1 on v0

v1 whole, which is shorter than its diff:
```python
import jax
import jax.numpy as jnp
from jax import lax
from jax.sharding import PartitionSpec as P

SWAP = ((0, 1), (1, 0))


def shift(step):
    return [(j, (j + step) % 16) for j in range(16)]


def swap(value):
    return lax.ppermute(value, "stream", SWAP)


def on_device(doubles, integrals, tiles):
    core = lax.axis_index("stream")
    mine = lax.dynamic_index_in_dim(doubles, core, 1, keepdims=False)
    first = lax.ppermute(mine, "vir", shift(1))
    second = lax.ppermute(mine, "vir", shift(8))
    used = tiles[0, 0]
    other_used = swap(used)
    blocks = integrals[0, 0]
    kept = lax.dynamic_index_in_dim(blocks, core, 0, keepdims=False)
    got = swap(lax.dynamic_index_in_dim(blocks, 1 - core, 0, keepdims=False))
    total = 0
    for slot, held in enumerate((first, second)):
        other = swap(held)
        for use, block in ((used[slot], kept[slot]), (other_used[slot], got[slot])):
            picked = jnp.where(use % 2 == core, held, other)
            total = total + lax.dot_general(
                picked, block, (((1,), (1,)), ((), ())), preferred_element_type=jnp.float32
            )
    return total.astype(jnp.bfloat16)[:, None]


def solution(mesh):
    placed = (
        P("occ", "vir", None),
        P("vir", "stream", None, None, None, None),
        P("vir", "stream", None),
    )
    return jax.shard_map(
        on_device,
        mesh=mesh,
        in_specs=placed,
        out_specs=P("occ", ("vir", "stream"), None),
        check_vma=False,
    )
```

time: 211 us -> 71.9 us (0.34)
  waiting for transfers between devices: 163 us -> 37.1 us
  blocking collectives: 12.8 us -> 0 us
  starting transfers between devices: 0.01 us -> 6.92 us
  local copies, waits for them, and re-layouts: 13.5 us -> 7.81 us
  between operations: 13.4 us -> 7.83 us
  matrix products: 8.54 us -> 11.9 us
    all_gather x1 -> x0, waiting for transfers between devices: 163 us -> none  [on_device(): whole = lax.all_gather(doubles, 'vir', axis=1, tiled=True)]
    ppermute x0 -> x6, waiting for transfers between devices: none -> 37.1 us  [the longest x1 37.1 us: on_device(): first = lax.ppermute(mine, 'vir', shift(1))]
    psum x1 -> x0, blocking collectives: 12.8 us -> none  [on_device(): summed = lax.psum(partial_value, 'stream')]
    gather x1 -> x0, local copies, waits for them, and re-layouts: 8.8 us -> none  [on_device(): picked = jnp.take(whole, used, axis=1)]
    ppermute x0 -> x6, starting transfers between devices: none -> 6.92 us  [the longest x4 4.55 us: swap(): return lax.ppermute(value, 'stream', SWAP)]
    squeeze x0 -> x1, local copies, waits for them, and re-layouts: none -> 4.72 us  [on_device(): got = swap(lax.dynamic_index_in_dim(blocks, 1 - core, 0, keepdims=False))]
    unnamed x3 -> x5, local copies, waits for them, and re-layouts: 3.71 us -> 0.28 us
    dot_general x1 -> x4, matrix products: 8.54 us -> 11.9 us  [on_device(): lax.dot_general(picked, block, (((1,), (1,)), ((), ())), preferred_elemen...]
  transfers between devices with their start and end apart: 1 -> 6, of which waited for: 1 -> 1; matrix products, arithmetic and copies ran while one was open for 0% -> 12% of each run, Pallas kernels for 0% -> 0%
where the time goes in v1:
time: 71.9 us; the launch traced here: 71.6 us
  waiting for transfers between devices  37.1 us (52%)
  matrix products  11.9 us (17%)
  between operations  7.83 us (11%)
  local copies, waits for them, and re-layouts  7.81 us (11%)
  starting transfers between devices  6.92 us (10%)
    ppermute x1, waiting for transfers between devices, on_device(): first = lax.ppermute(mine, 'vir', shift(1))  37.1 us
    dot_general x4, matrix products, on_device(): lax.dot_general(picked, block, (((1,), (1,)), ((), ())), preferred_elemen...  11.9 us
    squeeze x1, local copies, waits for them, and re-layouts, on_device(): got = swap(lax.dynamic_index_in_dim(blocks, 1 - core, 0, keepdims=False))  4.72 us
    ppermute x4, starting transfers between devices, swap(): return lax.ppermute(value, 'stream', SWAP)  4.55 us
    ppermute x1, starting transfers between devices, on_device(): second = lax.ppermute(mine, 'vir', shift(8))  2.29 us
    dynamic_slice x1, local copies, waits for them, and re-layouts, on_device(): mine = lax.dynamic_index_in_dim(doubles, core, 1, keepdims=False)  1.62 us
  transfers between devices with their start and end apart: 6, of which 1 were waited for; matrix products, arithmetic and copies ran while one was open for 12% of the time, Pallas kernels for 0%

profile of v1, /device:TPU:1, one launch (start us, length us, event | category | flops | bytes accessed | tf_op | source)
XLA Modules:
  0.0 71.6 jit_solution(2083259893229767257)
XLA Ops:
  0.0 0.0 copy-start
  0.0 4.7 %dynamic-slice_bitcast_fusion = bf16[2,1024,1024]{2,1,0:T(8,128)(2,1)} fusion(bf16[1,1,2,2,1024,1024]{5,4,3,2,1,0:T(8,128)(2,1)} %param.4, s32[]{:T(128)S(6)} %select_n.61), kind=kLoop, calls=%fused_computation | loop fusion | bytes 8388612 | tf_op jit(solution)/shard_map/jit(dynamic_index_in_dim)/squeeze | solution.py:26
  4.7 3.2 %collective-permute-start.3 = (bf16[2,1024,1024]{2,1,0:T(8,128)(2,1)}, bf16[2,1024,1024]{2,1,0:T(8,128)(2,1)}, u32[]{:S(2)}, u32[]{:S(2)}) collective-permute-start(bf16[2,1024,1024]{2,1,0:T(8,128)(2,1)} %dynamic-slice_bitcast_fusion), channel_id=1, source_target_pairs={{0,1},{1,0},{2,3},{3,2},{4,5},{5,4},{6,7},{7,6},{8,9},{9,8},{10,11... | collective-permute-start | bytes 12582920 | tf_op jit(solution)/shard_map/ppermute | solution.py:14
  8.0 0.0 copy-done
  8.0 1.6 %constant_dynamic-slice_fusion = bf16[384,1,1024]{2,1,0:T(2,128)(2,1)S(1)} fusion(bf16[384,2,1024]{2,1,0:T(2,128)(2,1)S(1)} %copy-done, s32[]{:T(128)S(6)} %select_n.56), kind=kLoop, calls=%fused_computation.22 | loop fusion | bytes 1572868 | tf_op jit(solution)/shard_map/jit(dynamic_index_in_dim)/dynamic_slice | solution.py:19
  9.6 0.3 copy.7
  9.9 0.1 collective-permute-start
  10.0 2.3 %collective-permute-start.4 = (bf16[384,1024]{1,0:T(8,128)(2,1)S(1)}, bf16[384,1024]{1,0:T(8,128)(2,1)S(1)}, u32[]{:S(2)}, u32[]{:S(2)}) collective-permute-start(bf16[384,1024]{1,0:T(8,128)(2,1)S(1)} %bitcast.27), channel_id=1, source_target_pairs={{0,16},{2,18},{4,20},{6,22},{8,24},{10,26},{12,28},{14,30},{16,0},... | collective-permute-start | bytes 2359304 | tf_op jit(solution)/shard_map/ppermute | solution.py:21
  12.3 37.1 %collective-permute-done = bf16[384,1024]{1,0:T(8,128)(2,1)} collective-permute-done((bf16[384,1024]{1,0:T(8,128)(2,1)S(1)}, bf16[384,1024]{1,0:T(8,128)(2,1)}, u32[]{:S(2)}, u32[]{:S(2)}) %collective-permute-start) | collective-permute-done | bytes 786464 | tf_op jit(solution)/shard_map/ppermute | solution.py:20
  49.4 0.8 %collective-permute-start.1 = (bf16[384,1024]{1,0:T(8,128)(2,1)}, bf16[384,1024]{1,0:T(8,128)(2,1)}, u32[]{:S(2)}, u32[]{:S(2)}) collective-permute-start(bf16[384,1024]{1,0:T(8,128)(2,1)} %collective-permute-done), channel_id=1, source_target_pairs={{0,1},{1,0},{2,3},{3,2},{4,5},{5,4},{6,7},{7,6},{8,9},{9,8},{10,11... | collective-permute-start | bytes 2359304 | tf_op jit(solution)/shard_map/ppermute | solution.py:14
  50.2 0.0 collective-permute-done.4
  50.2 0.0 collective-permute-start.5
  50.2 0.0 copy-done.1
  50.2 0.5 collective-permute-start.2
  50.7 0.6 fusion.18
  55.2 0.0 collective-permute-done.2
  55.2 0.6 fusion.17
  59.7 0.0 collective-permute-done.1
  59.7 2.9 %fusion.3 = f32[384,1024]{1,0:T(8,128)S(1)} fusion(bf16[1,1,2,2,1024,1024]{5,4,3,2,1,0:T(8,128)(2,1)} %param.4, s32[]{:T(128)S(6)} %select_n.56, bf16[384,1024]{1,0:T(8,128)(2,1)} %collective-permute-done, bf16[384,1024]{1,0:T(8,128)(2,1)} %collective-permute-done.1, pred[]{:T(512)S(6)} %eq.17), kind=kOutput, calls=%fused_computation.8 | convolution fusion | flops 805699584 | bytes 5242885 | tf_op jit(solution)/shard_map/dot_general | solution.py:32
  62.5 0.0 collective-permute-done.5
  62.6 2.6 %fusion.1 = f32[384,1024]{1,0:T(8,128)S(1)} fusion(bf16[1,1,2,2,1024,1024]{5,4,3,2,1,0:T(8,128)(2,1)} %param.4, s32[]{:T(128)S(6)} %select_n.56, s32[]{:T(128)S(6)} %add.41, bf16[384,1024]{1,0:T(8,128)(2,1)S(1)} %collective-permute-done.4, bf16[384,1024]{1,0:T(8,128)(2,1)S(1)} %collective-permute-done.5, pred[]{:T(512)S(6)} %eq.19), kind=kOutput, calls=%fused_computation.4 | convolution fusion | flops 805699584 | bytes 5242889 | tf_op jit(solution)/shard_map/dot_general | solution.py:32
  65.2 0.0 collective-permute-done.3
  65.2 2.9 %fusion.2 = f32[384,1024]{1,0:T(8,128)S(1)} fusion(bf16[2,1024,1024]{2,1,0:T(8,128)(2,1)} %collective-permute-done.3, bf16[384,1024]{1,0:T(8,128)(2,1)} %collective-permute-done, bf16[384,1024]{1,0:T(8,128)(2,1)} %collective-permute-done.1, pred[]{:T(512)S(6)} %eq.18), kind=kOutput, calls=%fused_computation.6 | convolution fusion | flops 805699584 | bytes 5242881 | tf_op jit(solution)/shard_map/dot_general | solution.py:32
  68.1 3.6 %fusion.4 = bf16[384,1,1024]{2,0,1:T(8,128)(2,1)} fusion(f32[384,1024]{1,0:T(8,128)S(1)} %fusion.1, f32[384,1024]{1,0:T(8,128)S(1)} %fusion.3, f32[384,1024]{1,0:T(8,128)S(1)} %fusion.2, bf16[2,1024,1024]{2,1,0:T(8,128)(2,1)} %collective-permute-done.3, bf16[384,1024]{1,0:T(8,128)(2,1)S(1)} %collective-permute-done.4, ...), kind=kOutput, calls=%fused_computation.10 | convolution fusion | flops 807272448 | bytes 9175041 | tf_op jit(solution)/shard_map/dot_general | solution.py:32
  (1 shorter events, 0.0 us)
Async XLA Ops:
  0.0 8.0 %copy-start = (bf16[384,2,1024]{2,1,0:T(2,128)(2,1)S(1)}, bf16[384,2,1024]{2,1,0:T(2,128)(2,1)}, u32[]{:S(2)}) copy-start(bf16[384,2,1024]{2,1,0:T(2,128)(2,1)} %param.3) | copy-start | bytes 4718596
  4.7 60.4 %collective-permute-start.3 = (bf16[2,1024,1024]{2,1,0:T(8,128)(2,1)}, bf16[2,1024,1024]{2,1,0:T(8,128)(2,1)}, u32[]{:S(2)}, u32[]{:S(2)}) collective-permute-start(bf16[2,1024,1024]{2,1,0:T(8,128)(2,1)} %dynamic-slice_bitcast_fusion), channel_id=1, source_target_pairs={{0,1},{1,0},{2,3},{3,2},{4,5},{5,4},{6,7},{7,6},{8,9},{9,8},{10,11... | collective-permute-start | bytes 12582920 | tf_op jit(solution)/shard_map/ppermute | solution.py:14
  8.0 42.2 %copy-start.1 = (s32[1,1,2]{2,1,0:T(1,128)S(1)}, s32[1,1,2]{2,1,0:T(1,128)}, u32[]{:S(2)}) copy-start(s32[1,1,2]{2,1,0:T(1,128)} %param.5) | copy-start | bytes 28
  9.9 39.5 %collective-permute-start = (bf16[384,1024]{1,0:T(8,128)(2,1)S(1)}, bf16[384,1024]{1,0:T(8,128)(2,1)}, u32[]{:S(2)}, u32[]{:S(2)}) collective-permute-start(bf16[384,1024]{1,0:T(8,128)(2,1)S(1)} %bitcast.26), channel_id=1, source_target_pairs={{0,2},{2,4},{4,6},{6,8},{8,10},{10,12},{12,14},{14,16},{16,18},{18... | collective-permute-start | bytes 2359304 | tf_op jit(solution)/shard_map/ppermute | solution.py:20
  10.0 40.2 %collective-permute-start.4 = (bf16[384,1024]{1,0:T(8,128)(2,1)S(1)}, bf16[384,1024]{1,0:T(8,128)(2,1)S(1)}, u32[]{:S(2)}, u32[]{:S(2)}) collective-permute-start(bf16[384,1024]{1,0:T(8,128)(2,1)S(1)} %bitcast.27), channel_id=1, source_target_pairs={{0,16},{2,18},{4,20},{6,22},{8,24},{10,26},{12,28},{14,30},{16,0},... | collective-permute-start | bytes 2359304 | tf_op jit(solution)/shard_map/ppermute | solution.py:21
  49.4 10.3 %collective-permute-start.1 = (bf16[384,1024]{1,0:T(8,128)(2,1)}, bf16[384,1024]{1,0:T(8,128)(2,1)}, u32[]{:S(2)}, u32[]{:S(2)}) collective-permute-start(bf16[384,1024]{1,0:T(8,128)(2,1)} %collective-permute-done), channel_id=1, source_target_pairs={{0,1},{1,0},{2,3},{3,2},{4,5},{5,4},{6,7},{7,6},{8,9},{9,8},{10,11... | collective-permute-start | bytes 2359304 | tf_op jit(solution)/shard_map/ppermute | solution.py:14
  50.2 12.4 %collective-permute-start.5 = (bf16[384,1024]{1,0:T(8,128)(2,1)S(1)}, bf16[384,1024]{1,0:T(8,128)(2,1)S(1)}, u32[]{:S(2)}, u32[]{:S(2)}) collective-permute-start(bf16[384,1024]{1,0:T(8,128)(2,1)S(1)} %collective-permute-done.4), channel_id=1, source_target_pairs={{0,1},{1,0},{2,3},{3,2},{4,5},{5,4},{6,7},{7,6},{8,9},{9,8},{10,11... | collective-permute-start | bytes 2359304 | tf_op jit(solution)/shard_map/ppermute | solution.py:14
  50.2 5.0 %collective-permute-start.2 = (s32[2]{0:T(128)S(1)}, s32[2]{0:T(128)S(1)}, u32[]{:S(2)}, u32[]{:S(2)}) collective-permute-start(s32[2]{0:T(128)S(1)} %bitcast.28), channel_id=1, source_target_pairs={{0,1},{1,0},{2,3},{3,2},{4,5},{5,4},{6,7},{7,6},{8,9},{9,8},{10,11... | collective-permute-start | bytes 32 | tf_op jit(solution)/shard_map/ppermute | solution.py:14

commit v2 on v0

v2 whole, which is shorter than its diff:
```python
import functools

import jax
import jax.numpy as jnp
from jax import lax
from jax.experimental import pallas as pl
from jax.experimental.pallas import tpu as pltpu
from jax.sharding import PartitionSpec as P

SWAP = ((0, 1), (1, 0))
CUT = 384
BUSY = 0
HOLD = 4600*10**6
TRANSPOSED = (((1,), (1,)), ((), ()))


def device(x, y, core):
    return ((x % 4) * 4 + y % 4) * 2 + core


def chips():
    return [(x, y) for x in range(4) for y in range(4)]


def route(pairs):
    return tuple((device(*a), device(*b)) for a, b in pairs)


ACROSS = route(((x, y, c), (x + 2, y, c)) for x, y in chips() for c in (0, 1))
WRAP = [((x, 3, c), (x + 1, 0, c)) for x in range(4) for c in (0, 1)]
INSIDE = [((x, y, c), (x, y + 1, c)) for x, y in chips() for c in (0, 1) if y < 3]
NEXT = route(INSIDE + WRAP)
NEXT_INSIDE = route(INSIDE)
RELAY_ROW = {0: 1, 1: 0}
RELAY_Y = route(((x, 3, c), (x, RELAY_ROW[c], c)) for x in range(4) for c in (0, 1))
RELAY_X = route(((x, RELAY_ROW[c], c), (x + 1, 0, c)) for x in range(4) for c in (0, 1))


def swap(value):
    return lax.ppermute(value, "stream", SWAP)


def send(value, pairs):
    return lax.ppermute(value, ("vir", "stream"), pairs)


VMEM = pl.BlockSpec(memory_space=pltpu.VMEM)
SMEM = pl.BlockSpec(memory_space=pltpu.SMEM)
ANYWHERE = pl.BlockSpec(memory_space=pl.ANY)


def params(mebibytes):
    return pltpu.CompilerParams(vmem_limit_bytes=mebibytes * 2**20)


def load_kernel(blocks, got, weights, arrived):
    core = lax.axis_index("stream")
    copies = [
        pltpu.make_async_copy(whole.at[core], weights.at[holder], arrived.at[holder])
        for holder, whole in enumerate((blocks, got))
    ]
    for copy in copies:
        copy.start()
    for copy in copies:
        copy.wait()


def load(blocks, got):
    hbm = pl.BlockSpec(memory_space=pltpu.HBM)
    return pl.pallas_call(
        load_kernel,
        out_shape=jax.ShapeDtypeStruct((2, 2, 1024, 1024), blocks.dtype),
        in_specs=[hbm, hbm],
        out_specs=VMEM,
        scratch_shapes=[pltpu.SemaphoreType.DMA((2,))],
        compiler_params=params(1),
    )(blocks, got)


def choose_kernel(inside, relayed, out, arrived):
    row = lax.axis_index("vir") % 4

    def move(source):
        copy = pltpu.make_async_copy(source, out, arrived)
        copy.start()
        copy.wait()

    @pl.when(row != 0)
    def _():
        move(inside)

    @pl.when(row == 0)
    def _():
        move(relayed)


def choose(inside, relayed):
    return pl.pallas_call(
        choose_kernel,
        out_shape=jax.ShapeDtypeStruct(inside.shape, inside.dtype),
        in_specs=[ANYWHERE] * 2,
        out_specs=VMEM,
        scratch_shapes=[pltpu.SemaphoreType.DMA],
        compiler_params=params(1),
    )(inside, relayed)


def hold_kernel(*refs):
    pass


def hold(*values, flops):
    return pl.pallas_call(
        hold_kernel,
        out_shape=[jax.ShapeDtypeStruct(value.shape, value.dtype) for value in values],
        in_specs=[ANYWHERE] * len(values),
        out_specs=[ANYWHERE] * len(values),
        input_output_aliases={i: i for i in range(len(values))},
        cost_estimate=pl.CostEstimate(flops=flops, bytes_accessed=0, transcendentals=0),
        compiler_params=params(1),
    )(*values)


def add_kernel(places, has_total, flags, weights, *refs):
    total = refs[-2][...] if has_total else None
    out = refs[-1]
    for holder in (0, 1):
        for i, (slot, low, high) in enumerate(places):
            held, other = refs[2 * i], refs[2 * i + 1]
            picked = jnp.where(flags[holder * 2 + slot] == 1, held[...], other[...])
            block = weights[holder, slot, :, low:high]
            term = lax.dot_general(picked, block, TRANSPOSED, preferred_element_type=jnp.float32)
            total = term if total is None else total + term
    out[...] = total.astype(out.dtype)


def add_parts(flags, weights, parts, total=None, dtype=jnp.float32, flops=0):
    operands = [flags, weights]
    for part in parts:
        operands += part[3:]
    if total is not None:
        operands.append(total)
    return pl.pallas_call(
        functools.partial(add_kernel, tuple(part[:3] for part in parts), total is not None),
        out_shape=jax.ShapeDtypeStruct((parts[0][3].shape[0], 1024), dtype),
        in_specs=[SMEM] + [VMEM] * (len(operands) - 1),
        out_specs=VMEM,
        cost_estimate=pl.CostEstimate(flops=flops, bytes_accessed=0, transcendentals=0),
        compiler_params=params(12),
    )(*operands)


def on_device(doubles, integrals, tiles):
    core = lax.axis_index("stream")
    mine = lax.dynamic_index_in_dim(doubles, core, 1, keepdims=False)
    left, right = mine[:, :CUT], mine[:, CUT:]
    across = send(mine, ACROSS)
    relayed = send(send(right, RELAY_Y), RELAY_X)
    inside = send(right, NEXT_INSIDE)
    first_left = send(left, NEXT)

    blocks, _ = lax.optimization_barrier((integrals[0, 0], mine))
    got, tiles = lax.optimization_barrier((swap(blocks), tiles))
    weights = load(blocks, got)
    used = tiles[0, 0]
    all_used = jnp.concatenate([used, swap(used)])
    flags = (all_used % 2 == core).astype(jnp.int32)

    across, inside, weights, flags = lax.optimization_barrier((across, inside, weights, flags))
    first_right = choose(inside, relayed)
    total = add_parts(flags, weights, [(1, 0, 1024, across, swap(across))], flops=BUSY)
    first_left, other_left = hold(first_left, swap(first_left), flops=HOLD)
    out = add_parts(
        flags,
        weights,
        [
            (0, 0, CUT, first_left, other_left),
            (0, CUT, 1024, first_right, swap(first_right)),
        ],
        total,
        jnp.bfloat16,
    )
    return out[:, None]


def solution(mesh):
    placed = (
        P("occ", "vir", None),
        P("vir", "stream", None, None, None, None),
        P("vir", "stream", None),
    )
    return jax.shard_map(
        on_device,
        mesh=mesh,
        in_specs=placed,
        out_specs=P("occ", ("vir", "stream"), None),
        check_vma=False,
    )
```

time: 211 us -> 42.6 us (0.20)
  waiting for transfers between devices: 163 us -> 14.9 us
  starting transfers between devices: 0.01 us -> 13.6 us
  between operations: 13.4 us -> 0.13 us
  blocking collectives: 12.8 us -> 0 us
  matrix products: 8.54 us -> 0 us
  Pallas kernels: 0 us -> 6.93 us
  local copies, waits for them, and re-layouts: 13.5 us -> 6.77 us
    all_gather x1 -> x0, waiting for transfers between devices: 163 us -> none  [on_device(): whole = lax.all_gather(doubles, 'vir', axis=1, tiled=True)]
    ppermute x0 -> x10, waiting for transfers between devices: none -> 14.9 us  [the longest x5 14.1 us: send(): return lax.ppermute(value, ('vir', 'stream'), pairs)]
    ppermute x0 -> x10, starting transfers between devices: none -> 13.6 us  [the longest x5 8.25 us: send(): return lax.ppermute(value, ('vir', 'stream'), pairs)]
    psum x1 -> x0, blocking collectives: 12.8 us -> none  [on_device(): summed = lax.psum(partial_value, 'stream')]
    gather x1 -> x0, local copies, waits for them, and re-layouts: 8.8 us -> none  [on_device(): picked = jnp.take(whole, used, axis=1)]
    dot_general x1 -> x0, matrix products: 8.54 us -> none  [on_device(): jnp.einsum('osq,aspq->oap', picked, integrals[0, 0], preferred_element_ty...]
    pallas_call x0 -> x5, Pallas kernels: none -> 6.93 us  [the longest x2 6.03 us: add_parts(): pl.pallas_call(functools.partial(add_kernel, tuple((part[:3] for part in...]
    unnamed x3 -> x7, local copies, waits for them, and re-layouts: 3.71 us -> 5.06 us
  transfers between devices with their start and end apart: 1 -> 10, of which waited for: 1 -> 4; matrix products, arithmetic and copies ran while one was open for 0% -> 0% of each run, Pallas kernels for 0% -> 8%
where the time goes in v2:
time: 42.6 us; the launch traced here: 42.4 us
  waiting for transfers between devices  14.9 us (35%)
  starting transfers between devices  13.6 us (32%)
  Pallas kernels  6.93 us (16%)
  local copies, waits for them, and re-layouts  6.77 us (16%)
    ppermute x5, waiting for transfers between devices, send(): return lax.ppermute(value, ('vir', 'stream'), pairs)  14.1 us
    ppermute x5, starting transfers between devices, send(): return lax.ppermute(value, ('vir', 'stream'), pairs)  8.25 us
    pallas_call x2, Pallas kernels, add_parts(): pl.pallas_call(functools.partial(add_kernel, tuple((part[:3] for part in...  6.03 us
    ppermute x5, starting transfers between devices, swap(): return lax.ppermute(value, 'stream', SWAP)  5.36 us
    unnamed x7, local copies, waits for them, and re-layouts  5.06 us
    dynamic_slice x1, local copies, waits for them, and re-layouts, on_device(): mine = lax.dynamic_index_in_dim(doubles, core, 1, keepdims=False)  1.62 us
  transfers between devices with their start and end apart: 10, of which 4 were waited for; matrix products, arithmetic and copies ran while one was open for 0% of the time, Pallas kernels for 8%

profile of v2, /device:TPU:1, one launch (start us, length us, event | category | flops | bytes accessed | tf_op | source)
XLA Modules:
  0.0 42.4 jit_solution(6155383633831406679)
XLA Ops:
  0.0 1.4 %copy-done = bf16[384,2,1024]{2,1,0:T(2,128)(2,1)S(1)} copy-done((bf16[384,2,1024]{2,1,0:T(2,128)(2,1)S(1)}, bf16[384,2,1024]{2,1,0:T(2,128)(2,1)}, u32[]{:S(2)}) %copy-start) | copy-done | bytes 1572888
  1.4 1.6 %constant_dynamic-slice_fusion = bf16[384,1,1024]{2,1,0:T(2,128)(2,1)S(1)} fusion(bf16[384,2,1024]{2,1,0:T(2,128)(2,1)S(1)} %copy-done, s32[]{:T(128)S(6)} %select_n.11), kind=kLoop, calls=%fused_computation.6 | loop fusion | bytes 1572868 | tf_op jit(solution)/shard_map/jit(dynamic_index_in_dim)/dynamic_slice | solution.py:155
  3.0 0.3 copy.9
  3.3 3.3 %collective-permute-start.2 = (bf16[2,2,1024,1024]{3,2,1,0:T(8,128)(2,1)}, bf16[2,2,1024,1024]{3,2,1,0:T(8,128)(2,1)S(1)}, u32[]{:S(2)}, u32[]{:S(2)}) collective-permute-start(bf16[2,2,1024,1024]{3,2,1,0:T(8,128)(2,1)} %bitcast.6), channel_id=1, source_target_pairs={{0,1},{1,0},{2,3},{3,2},{4,5},{5,4},{6,7},{7,6},{8,9},{9,8},{10,11... | collective-permute-start | bytes 25165832 | tf_op jit(solution)/shard_map/ppermute | solution.py:40
  6.7 1.0 %collective-permute-start = (bf16[384,1024]{1,0:T(8,128)(2,1)S(1)}, bf16[384,1024]{1,0:T(8,128)(2,1)S(1)}, u32[]{:S(2)}, u32[]{:S(2)}) collective-permute-start(bf16[384,1024]{1,0:T(8,128)(2,1)S(1)} %bitcast.8), channel_id=1, source_target_pairs={{0,16},{1,17},{2,18},{3,19},{4,20},{5,21},{6,22},{7,23},{8,24},{9,... | collective-permute-start | bytes 2359304 | tf_op jit(solution)/shard_map/ppermute | solution.py:44
  7.7 0.1 slice.8
  7.7 1.3 %collective-permute-start.6 = (bf16[384,640]{1,0:T(8,128)(2,1)S(1)}, bf16[384,640]{1,0:T(8,128)(2,1)S(1)}, u32[]{:S(2)}, u32[]{:S(2)}) collective-permute-start(bf16[384,640]{1,0:T(8,128)(2,1)S(1)} %slice.8), channel_id=1, source_target_pairs={{6,2},{7,1},{14,10},{15,9},{22,18},{23,17},{30,26},{31,25},{38,34}... | collective-permute-start | bytes 1474568 | tf_op jit(solution)/shard_map/ppermute | solution.py:44
  9.0 2.6 %collective-permute-start.1 = (bf16[384,640]{1,0:T(8,128)(2,1)S(1)}, bf16[384,640]{1,0:T(8,128)(2,1)S(1)}, u32[]{:S(2)}, u32[]{:S(2)}) collective-permute-start(bf16[384,640]{1,0:T(8,128)(2,1)S(1)} %slice.8), channel_id=1, source_target_pairs={{0,2},{1,3},{2,4},{3,5},{4,6},{5,7},{8,10},{9,11},{10,12},{11,13},... | collective-permute-start | bytes 1474568 | tf_op jit(solution)/shard_map/ppermute | solution.py:44
  11.7 1.3 %collective-permute-start.4 = (bf16[384,384]{1,0:T(8,128)(2,1)S(1)}, bf16[384,384]{1,0:T(8,128)(2,1)S(1)}, u32[]{:S(2)}, u32[]{:S(2)}) collective-permute-start(bf16[384,384]{1,0:T(8,128)(2,1)S(1)} %slice.9), channel_id=1, source_target_pairs={{0,2},{1,3},{2,4},{3,5},{4,6},{5,7},{8,10},{9,11},{10,12},{11,13},... | collective-permute-start | bytes 884744 | tf_op jit(solution)/shard_map/ppermute | solution.py:44
  13.1 5.9 %collective-permute-done.6 = bf16[384,640]{1,0:T(8,128)(2,1)S(1)} collective-permute-done((bf16[384,640]{1,0:T(8,128)(2,1)S(1)}, bf16[384,640]{1,0:T(8,128)(2,1)S(1)}, u32[]{:S(2)}, u32[]{:S(2)}) %collective-permute-start.6) | collective-permute-done | bytes 491552 | tf_op jit(solution)/shard_map/ppermute | solution.py:44
  18.9 2.0 %collective-permute-start.7 = (bf16[384,640]{1,0:T(8,128)(2,1)S(1)}, bf16[384,640]{1,0:T(8,128)(2,1)S(1)}, u32[]{:S(2)}, u32[]{:S(2)}) collective-permute-start(bf16[384,640]{1,0:T(8,128)(2,1)S(1)} %collective-permute-done.6), channel_id=1, source_target_pairs={{2,8},{1,9},{10,16},{9,17},{18,24},{17,25},{26,0},{25,1},{34,40},{... | collective-permute-start | bytes 1474568 | tf_op jit(solution)/shard_map/ppermute | solution.py:44
  20.9 0.1 collective-permute-start.3
  21.0 3.4 %copy-done.1 = bf16[1,1,2,2,1024,1024]{5,4,3,2,1,0:T(8,128)(2,1)S(1)} copy-done((bf16[1,1,2,2,1024,1024]{5,4,3,2,1,0:T(8,128)(2,1)S(1)}, bf16[1,1,2,2,1024,1024]{5,4,3,2,1,0:T(8,128)(2,1)}, u32[]{:S(2)}) %copy-start.1) | copy-done | bytes 8388632
  24.4 0.6 %shard_map.37.weights = bf16[2,2,1024,1024]{3,2,1,0:T(8,128)(2,1)S(1)} custom-call(bf16[2,2,1024,1024]{3,2,1,0:T(8,128)(2,1)S(1)} %bitcast.7, bf16[2,2,1024,1024]{3,2,1,0:T(8,128)(2,1)S(1)} %collective-permute-done.2.got), custom_call_target="tpu_custom_call" | custom-call | tf_op jit(solution)/shard_map/pallas_call | solution.py:70
  25.0 0.1 compare_convert_fusion.flags
  25.1 2.2 %collective-permute-done.refs_0_ = bf16[384,1024]{1,0:T(8,128)(2,1)S(1)} collective-permute-done((bf16[384,1024]{1,0:T(8,128)(2,1)S(1)}, bf16[384,1024]{1,0:T(8,128)(2,1)S(1)}, u32[]{:S(2)}, u32[]{:S(2)}) %collective-permute-start) | collective-permute-done | bytes 786464 | tf_op jit(solution)/shard_map/ppermute | solution.py:44
  27.3 1.3 %collective-permute-start.9 = (bf16[384,1024]{1,0:T(8,128)(2,1)S(1)}, bf16[384,1024]{1,0:T(8,128)(2,1)S(1)}, u32[]{:S(2)}, u32[]{:S(2)}) collective-permute-start(bf16[384,1024]{1,0:T(8,128)(2,1)S(1)} %collective-permute-done.refs_0_), channel_id=1, source_target_pairs={{0,1},{1,0},{2,3},{3,2},{4,5},{5,4},{6,7},{7,6},{8,9},{9,8},{10,11... | collective-permute-start | bytes 2359304 | tf_op jit(solution)/shard_map/ppermute | solution.py:40
  28.7 6.0 %collective-permute-done.4.refs_0_ = bf16[384,384]{1,0:T(8,128)(2,1)S(1)} collective-permute-done((bf16[384,384]{1,0:T(8,128)(2,1)S(1)}, bf16[384,384]{1,0:T(8,128)(2,1)S(1)}, u32[]{:S(2)}, u32[]{:S(2)}) %collective-permute-start.4) | collective-permute-done | bytes 294944 | tf_op jit(solution)/shard_map/ppermute | solution.py:44
  34.7 0.5 %collective-permute-start.5 = (bf16[384,384]{1,0:T(8,128)(2,1)S(1)}, bf16[384,384]{1,0:T(8,128)(2,1)S(1)}, u32[]{:S(2)}, u32[]{:S(2)}) collective-permute-start(bf16[384,384]{1,0:T(8,128)(2,1)S(1)} %collective-permute-done.4.refs_0_), channel_id=1, source_target_pairs={{0,1},{1,0},{2,3},{3,2},{4,5},{5,4},{6,7},{7,6},{8,9},{9,8},{10,11... | collective-permute-start | bytes 884744 | tf_op jit(solution)/shard_map/ppermute | solution.py:40
  35.2 0.3 shard_map.39.refs_2_
  35.5 0.1 collective-permute-start.8
  35.6 0.8 %collective-permute-done.5.refs_1_ = bf16[384,384]{1,0:T(8,128)(2,1)S(1)} collective-permute-done((bf16[384,384]{1,0:T(8,128)(2,1)S(1)}, bf16[384,384]{1,0:T(8,128)(2,1)S(1)}, u32[]{:S(2)}, u32[]{:S(2)}) %collective-permute-start.5) | collective-permute-done | bytes 294944 | tf_op jit(solution)/shard_map/ppermute | solution.py:40
  36.4 2.4 %shard_map.40.refs_4_ = f32[384,1024]{1,0:T(8,128)S(1)} custom-call(s32[4]{0:T(128)S(1)} %compare_convert_fusion.flags, bf16[2,2,1024,1024]{3,2,1,0:T(8,128)(2,1)S(1)} %shard_map.37.weights, bf16[384,1024]{1,0:T(8,128)(2,1)S(1)} %collective-permute-done.refs_0_, bf16[384,1024]{1,0:T(8,128)(2,1)S(1)} %collective-permute-done.9.refs_1_), custom_call_target="tpu_custom_call" | custom-call | tf_op jit(solution)/shard_map/pallas_call | solution.py:143
  38.8 3.7 %shard_map.41 = bf16[384,1024]{1,0:T(8,128)(2,1)} custom-call(s32[4]{0:T(128)S(1)} %compare_convert_fusion.flags, bf16[2,2,1024,1024]{3,2,1,0:T(8,128)(2,1)S(1)} %shard_map.37.weights, bf16[384,384]{1,0:T(8,128)(2,1)S(1)} %get-tuple-element.19.refs_0_, bf16[384,384]{1,0:T(8,128)(2,1)S(1)} %get-tuple-element.20.refs_1_, ...), custom_call_target="tpu_custom_call" | custom-call | tf_op jit(solution)/shard_map/pallas_call | solution.py:143
  (12 shorter events, 0.1 us)
Async XLA Ops:
  0.0 1.4 %copy-start = (bf16[384,2,1024]{2,1,0:T(2,128)(2,1)S(1)}, bf16[384,2,1024]{2,1,0:T(2,128)(2,1)}, u32[]{:S(2)}) copy-start(bf16[384,2,1024]{2,1,0:T(2,128)(2,1)} %param.3) | copy-start | bytes 4718596
  3.0 17.9 %copy-start.2 = (s32[1,1,2]{2,1,0:T(1,128)S(1)}, s32[1,1,2]{2,1,0:T(1,128)}, u32[]{:S(2)}) copy-start(s32[1,1,2]{2,1,0:T(1,128)} %param.5) | copy-start | bytes 28
  3.3 17.6 %collective-permute-start.2 = (bf16[2,2,1024,1024]{3,2,1,0:T(8,128)(2,1)}, bf16[2,2,1024,1024]{3,2,1,0:T(8,128)(2,1)S(1)}, u32[]{:S(2)}, u32[]{:S(2)}) collective-permute-start(bf16[2,2,1024,1024]{3,2,1,0:T(8,128)(2,1)} %bitcast.6), channel_id=1, source_target_pairs={{0,1},{1,0},{2,3},{3,2},{4,5},{5,4},{6,7},{7,6},{8,9},{9,8},{10,11... | collective-permute-start | bytes 25165832 | tf_op jit(solution)/shard_map/ppermute | solution.py:40
  6.7 20.7 %collective-permute-start = (bf16[384,1024]{1,0:T(8,128)(2,1)S(1)}, bf16[384,1024]{1,0:T(8,128)(2,1)S(1)}, u32[]{:S(2)}, u32[]{:S(2)}) collective-permute-start(bf16[384,1024]{1,0:T(8,128)(2,1)S(1)} %bitcast.8), channel_id=1, source_target_pairs={{0,16},{1,17},{2,18},{3,19},{4,20},{5,21},{6,22},{7,23},{8,24},{9,... | collective-permute-start | bytes 2359304 | tf_op jit(solution)/shard_map/ppermute | solution.py:44
  7.7 11.2 %collective-permute-start.6 = (bf16[384,640]{1,0:T(8,128)(2,1)S(1)}, bf16[384,640]{1,0:T(8,128)(2,1)S(1)}, u32[]{:S(2)}, u32[]{:S(2)}) collective-permute-start(bf16[384,640]{1,0:T(8,128)(2,1)S(1)} %slice.8), channel_id=1, source_target_pairs={{6,2},{7,1},{14,10},{15,9},{22,18},{23,17},{30,26},{31,25},{38,34}... | collective-permute-start | bytes 1474568 | tf_op jit(solution)/shard_map/ppermute | solution.py:44
  9.0 16.0 %collective-permute-start.1 = (bf16[384,640]{1,0:T(8,128)(2,1)S(1)}, bf16[384,640]{1,0:T(8,128)(2,1)S(1)}, u32[]{:S(2)}, u32[]{:S(2)}) collective-permute-start(bf16[384,640]{1,0:T(8,128)(2,1)S(1)} %slice.8), channel_id=1, source_target_pairs={{0,2},{1,3},{2,4},{3,5},{4,6},{5,7},{8,10},{9,11},{10,12},{11,13},... | collective-permute-start | bytes 1474568 | tf_op jit(solution)/shard_map/ppermute | solution.py:44
  11.7 23.0 %collective-permute-start.4 = (bf16[384,384]{1,0:T(8,128)(2,1)S(1)}, bf16[384,384]{1,0:T(8,128)(2,1)S(1)}, u32[]{:S(2)}, u32[]{:S(2)}) collective-permute-start(bf16[384,384]{1,0:T(8,128)(2,1)S(1)} %slice.9), channel_id=1, source_target_pairs={{0,2},{1,3},{2,4},{3,5},{4,6},{5,7},{8,10},{9,11},{10,12},{11,13},... | collective-permute-start | bytes 884744 | tf_op jit(solution)/shard_map/ppermute | solution.py:44
  18.9 16.3 %collective-permute-start.7 = (bf16[384,640]{1,0:T(8,128)(2,1)S(1)}, bf16[384,640]{1,0:T(8,128)(2,1)S(1)}, u32[]{:S(2)}, u32[]{:S(2)}) collective-permute-start(bf16[384,640]{1,0:T(8,128)(2,1)S(1)} %collective-permute-done.6), channel_id=1, source_target_pairs={{2,8},{1,9},{10,16},{9,17},{18,24},{17,25},{26,0},{25,1},{34,40},{... | collective-permute-start | bytes 1474568 | tf_op jit(solution)/shard_map/ppermute | solution.py:44
  20.9 4.1 %collective-permute-start.3 = (s32[2]{0:T(128)S(1)}, s32[2]{0:T(128)S(1)}, u32[]{:S(2)}, u32[]{:S(2)}) collective-permute-start(s32[2]{0:T(128)S(1)} %bitcast.11), channel_id=1, source_target_pairs={{0,1},{1,0},{2,3},{3,2},{4,5},{5,4},{6,7},{7,6},{8,9},{9,8},{10,11... | collective-permute-start | bytes 32 | tf_op jit(solution)/shard_map/ppermute | solution.py:40
  21.0 3.4 %copy-start.1 = (bf16[1,1,2,2,1024,1024]{5,4,3,2,1,0:T(8,128)(2,1)S(1)}, bf16[1,1,2,2,1024,1024]{5,4,3,2,1,0:T(8,128)(2,1)}, u32[]{:S(2)}) copy-start(bf16[1,1,2,2,1024,1024]{5,4,3,2,1,0:T(8,128)(2,1)} %param.4) | copy-start | bytes 25165828
  27.3 9.1 %collective-permute-start.9 = (bf16[384,1024]{1,0:T(8,128)(2,1)S(1)}, bf16[384,1024]{1,0:T(8,128)(2,1)S(1)}, u32[]{:S(2)}, u32[]{:S(2)}) collective-permute-start(bf16[384,1024]{1,0:T(8,128)(2,1)S(1)} %collective-permute-done.refs_0_), channel_id=1, source_target_pairs={{0,1},{1,0},{2,3},{3,2},{4,5},{5,4},{6,7},{7,6},{8,9},{9,8},{10,11... | collective-permute-start | bytes 2359304 | tf_op jit(solution)/shard_map/ppermute | solution.py:40
  34.7 1.7 %collective-permute-start.5 = (bf16[384,384]{1,0:T(8,128)(2,1)S(1)}, bf16[384,384]{1,0:T(8,128)(2,1)S(1)}, u32[]{:S(2)}, u32[]{:S(2)}) collective-permute-start(bf16[384,384]{1,0:T(8,128)(2,1)S(1)} %collective-permute-done.4.refs_0_), channel_id=1, source_target_pairs={{0,1},{1,0},{2,3},{3,2},{4,5},{5,4},{6,7},{7,6},{8,9},{9,8},{10,11... | collective-permute-start | bytes 884744 | tf_op jit(solution)/shard_map/ppermute | solution.py:40
  35.5 3.2 %collective-permute-start.8 = (bf16[384,640]{1,0:T(8,128)(2,1)S(1)}, bf16[384,640]{1,0:T(8,128)(2,1)S(1)}, u32[]{:S(2)}, u32[]{:S(2)}) collective-permute-start(bf16[384,640]{1,0:T(8,128)(2,1)S(1)} %shard_map.39.refs_2_), channel_id=1, source_target_pairs={{0,1},{1,0},{2,3},{3,2},{4,5},{5,4},{6,7},{7,6},{8,9},{9,8},{10,11... | collective-permute-start | bytes 1474568 | tf_op jit(solution)/shard_map/ppermute | solution.py:40

commit v3 on v2

v3 whole, which is shorter than its diff:
```python
import functools

import jax
import jax.numpy as jnp
from jax import lax
from jax.experimental import pallas as pl
from jax.experimental.pallas import tpu as pltpu
from jax.sharding import PartitionSpec as P

SWAP = ((0, 1), (1, 0))
CUT = 256
SEPARATE = 4600 * 10**6
HOLD = 4600 * 10**6
TRANSPOSED = (((1,), (1,)), ((), ()))


def device(x, y, core):
    return ((x % 4) * 4 + y % 4) * 2 + core


def chips():
    return [(x, y) for x in range(4) for y in range(4)]


def route(pairs):
    return tuple((device(*a), device(*b)) for a, b in pairs)


ACROSS = route(((x, y, c), (x + 2, y, c)) for x, y in chips() for c in (0, 1))
WRAP = [((x, 3, c), (x + 1, 0, c)) for x in range(4) for c in (0, 1)]
INSIDE = [((x, y, c), (x, y + 1, c)) for x, y in chips() for c in (0, 1) if y < 3]
NEXT = route(INSIDE + WRAP)
NEXT_INSIDE = route(INSIDE)
RELAY_ROW = {0: 1, 1: 0}
RELAY_Y = route(((x, 3, c), (x, RELAY_ROW[c], c)) for x in range(4) for c in (0, 1))
RELAY_X = route(((x, RELAY_ROW[c], c), (x + 1, 0, c)) for x in range(4) for c in (0, 1))


def swap(value):
    return lax.ppermute(value, "stream", SWAP)


def send(value, pairs):
    return lax.ppermute(value, ("vir", "stream"), pairs)


VMEM = pl.BlockSpec(memory_space=pltpu.VMEM)
SMEM = pl.BlockSpec(memory_space=pltpu.SMEM)
ANYWHERE = pl.BlockSpec(memory_space=pl.ANY)


def params(mebibytes):
    return pltpu.CompilerParams(vmem_limit_bytes=mebibytes * 2**20)


def in_hbm(value):
    return pltpu.with_memory_space_constraint(value, pltpu.HBM)


def cut_kernel(doubles, out, arrived):
    rows = out.shape[0]
    core = lax.axis_index("stream")
    copy = pltpu.make_async_copy(doubles.at[pl.ds(core * rows, rows)], out, arrived)
    copy.start()
    copy.wait()


def cut_rows(doubles):
    shape = (doubles.shape[0] // 2, *doubles.shape[1:])
    return pl.pallas_call(
        cut_kernel,
        out_shape=jax.ShapeDtypeStruct(shape, doubles.dtype),
        in_specs=[pl.BlockSpec(memory_space=pltpu.HBM)],
        out_specs=VMEM,
        scratch_shapes=[pltpu.SemaphoreType.DMA],
        compiler_params=params(1),
    )(in_hbm(doubles))


def take_kernel(doubles, left, right):
    def take_pair(pair):
        left[...] = doubles[:, pair, :CUT]
        right[...] = doubles[:, pair, CUT:]

    @pl.when(lax.axis_index("stream") == 0)
    def _():
        take_pair(0)

    @pl.when(lax.axis_index("stream") == 1)
    def _():
        take_pair(1)


def take(doubles):
    rows, _, width = doubles.shape
    return pl.pallas_call(
        take_kernel,
        out_shape=[
            jax.ShapeDtypeStruct((rows, columns), doubles.dtype) for columns in (CUT, width - CUT)
        ],
        in_specs=[VMEM],
        out_specs=[VMEM] * 2,
        cost_estimate=pl.CostEstimate(flops=0, bytes_accessed=0, transcendentals=0),
        compiler_params=params(4),
    )(doubles)


def separate_kernel(pairs, out):
    rows = pairs.shape[0]
    out[:rows] = pairs[:, 0, :]
    out[rows:] = pairs[:, 1, :]


def separate(pairs):
    rows, count, width = pairs.shape
    return pl.pallas_call(
        separate_kernel,
        out_shape=jax.ShapeDtypeStruct((rows * count, width), pairs.dtype),
        in_specs=[VMEM],
        out_specs=VMEM,
        cost_estimate=pl.CostEstimate(flops=SEPARATE, bytes_accessed=0, transcendentals=0),
        compiler_params=params(4),
    )(pairs)


def keep_kernel(blocks, out, arrived):
    copy = pltpu.make_async_copy(blocks.at[lax.axis_index("stream")], out, arrived)
    copy.start()
    copy.wait()


def keep(blocks):
    return pl.pallas_call(
        keep_kernel,
        out_shape=jax.ShapeDtypeStruct(blocks.shape[1:], blocks.dtype),
        in_specs=[pl.BlockSpec(memory_space=pltpu.HBM)],
        out_specs=VMEM,
        scratch_shapes=[pltpu.SemaphoreType.DMA],
        compiler_params=params(1),
    )(in_hbm(blocks))


def choose_kernel(inside, relayed, out, arrived):
    row = lax.axis_index("vir") % 4

    def move(source):
        copy = pltpu.make_async_copy(source, out, arrived)
        copy.start()
        copy.wait()

    @pl.when(row != 0)
    def _():
        move(inside)

    @pl.when(row == 0)
    def _():
        move(relayed)


def choose(inside, relayed):
    return pl.pallas_call(
        choose_kernel,
        out_shape=jax.ShapeDtypeStruct(inside.shape, inside.dtype),
        in_specs=[ANYWHERE] * 2,
        out_specs=VMEM,
        scratch_shapes=[pltpu.SemaphoreType.DMA],
        compiler_params=params(1),
    )(inside, relayed)


def hold_kernel(*refs):
    pass


def hold(*values, flops):
    return pl.pallas_call(
        hold_kernel,
        out_shape=[jax.ShapeDtypeStruct(value.shape, value.dtype) for value in values],
        in_specs=[ANYWHERE] * len(values),
        out_specs=[ANYWHERE] * len(values),
        input_output_aliases={i: i for i in range(len(values))},
        cost_estimate=pl.CostEstimate(flops=flops, bytes_accessed=0, transcendentals=0),
        compiler_params=params(1),
    )(*values)


def multiply(picked, block):
    return lax.dot_general(picked, block, TRANSPOSED, preferred_element_type=jnp.float32)


def sum_call(kernel, dtype, flags, *operands):
    rows = operands[-1].shape[0]
    return pl.pallas_call(
        kernel,
        out_shape=jax.ShapeDtypeStruct((rows, 1024), dtype),
        in_specs=[SMEM] + [VMEM] * len(operands),
        out_specs=VMEM,
        cost_estimate=pl.CostEstimate(flops=0, bytes_accessed=0, transcendentals=0),
        compiler_params=params(12),
    )(flags, *operands)


def across_kernel(parity, kept, got, mine, other, out):
    core = lax.axis_index("stream")
    rows = mine.shape[0] // 2
    total = 0
    for holder, block in ((0, kept[1]), (1, got[core, 1])):
        second = parity[holder * 2 + 1] == 1
        halves = [jnp.where(second, half[rows:], half[:rows]) for half in (mine, other)]
        upper = jnp.where(core == 0, halves[0], halves[1])
        lower = jnp.where(core == 0, halves[1], halves[0])
        total = total + multiply(jnp.concatenate([upper, lower], 0), block)
    out[...] = total


def next_kernel(parity, kept, got, left, other_left, right, other_right, total, out):
    core = lax.axis_index("stream")
    result = total[...]
    for holder, block in ((0, kept[0]), (1, got[core, 0])):
        own = parity[holder * 2] == core
        picked = [
            jnp.where(own, held[...], swapped[...])
            for held, swapped in ((left, other_left), (right, other_right))
        ]
        result = result + multiply(jnp.concatenate(picked, 1), block)
    out[...] = result.astype(out.dtype)


def on_device(doubles, integrals, tiles):
    doubles, rows = lax.optimization_barrier((doubles, cut_rows(doubles)))
    across = send(rows, ACROSS)
    left, right = take(doubles)
    used = tiles[0, 0]
    parity = jnp.concatenate([used, swap(used)]) % 2
    relayed, parity = lax.optimization_barrier((send(right, RELAY_Y), parity))
    relayed = send(relayed, RELAY_X)
    inside = send(right, NEXT_INSIDE)
    first_left = send(left, NEXT)

    blocks, _ = lax.optimization_barrier((integrals[0, 0], rows))
    got = swap(blocks)
    kept = keep(blocks)
    across, inside, kept, got = lax.optimization_barrier((across, inside, kept, got))
    across = separate(across)
    total = sum_call(across_kernel, jnp.float32, parity, kept, got, across, swap(across))
    first_right = choose(inside, relayed)
    first_left, other_left = hold(first_left, swap(first_left), flops=HOLD)
    out = sum_call(
        next_kernel,
        jnp.bfloat16,
        parity,
        kept,
        got,
        first_left,
        other_left,
        first_right,
        swap(first_right),
        total,
    )
    return out[:, None]


def solution(mesh):
    placed = (
        P("occ", "vir", None),
        P("vir", "stream", None, None, None, None),
        P("vir", "stream", None),
    )
    return jax.shard_map(
        on_device,
        mesh=mesh,
        in_specs=placed,
        out_specs=P("occ", ("vir", "stream"), None),
        check_vma=False,
    )
```

time: 42.6 us -> 39.9 us (0.937)
  Pallas kernels: 6.93 us -> 12.6 us
  local copies, waits for them, and re-layouts: 6.77 us -> 1.41 us
  waiting for transfers between devices: 14.9 us -> 9.84 us
  starting transfers between devices: 13.6 us -> 15.7 us
    pallas_call x3 -> x6, Pallas kernels: 6.61 us -> 12.5 us  [the longest x2 5.66 us: sum_call(): pl.pallas_call(kernel, out_shape=jax.ShapeDtypeStruct((rows, 1024), dtype...]
    ppermute x5, waiting for transfers between devices: 14.1 us -> 8.5 us  [send(): return lax.ppermute(value, ('vir', 'stream'), pairs)]
    unnamed x7 -> x4, local copies, waits for them, and re-layouts: 5.06 us -> 1.41 us
    ppermute x5, starting transfers between devices: 5.36 us -> 8.63 us  [swap(): return lax.ppermute(value, 'stream', SWAP)]
    dynamic_slice x1 -> x0, local copies, waits for them, and re-layouts: 1.62 us -> none  [on_device(): mine = lax.dynamic_index_in_dim(doubles, core, 1, keepdims=False)]
    ppermute x5, starting transfers between devices: 8.25 us -> 7.02 us  [send(): return lax.ppermute(value, ('vir', 'stream'), pairs)]
    ppermute x5, waiting for transfers between devices: 0.79 us -> 1.34 us  [swap(): return lax.ppermute(value, 'stream', SWAP)]
  transfers between devices with their start and end apart: 10 -> 10, of which waited for: 4 -> 6; matrix products, arithmetic and copies ran while one was open for 0% -> 0% of each run, Pallas kernels for 8% -> 21%
where the time goes in v3:
time: 39.9 us; the launch traced here: 39.7 us
  starting transfers between devices  15.7 us (39%)
  Pallas kernels  12.6 us (32%)
  waiting for transfers between devices  9.84 us (25%)
  local copies, waits for them, and re-layouts  1.41 us (4%)
    ppermute x5, starting transfers between devices, swap(): return lax.ppermute(value, 'stream', SWAP)  8.63 us
    ppermute x5, waiting for transfers between devices, send(): return lax.ppermute(value, ('vir', 'stream'), pairs)  8.5 us
    ppermute x5, starting transfers between devices, send(): return lax.ppermute(value, ('vir', 'stream'), pairs)  7.02 us
    pallas_call x2, Pallas kernels, sum_call(): pl.pallas_call(kernel, out_shape=jax.ShapeDtypeStruct((rows, 1024), dtype...  5.66 us
    pallas_call x1, Pallas kernels, keep(): pl.pallas_call(keep_kernel, out_shape=jax.ShapeDtypeStruct(blocks.shape[1...  2.2 us
    pallas_call x1, Pallas kernels, take(): pl.pallas_call(take_kernel, out_shape=[jax.ShapeDtypeStruct((rows, column...  1.74 us
    pallas_call x1, Pallas kernels, separate(): pl.pallas_call(separate_kernel, out_shape=jax.ShapeDtypeStruct((rows * co...  1.73 us
    unnamed x4, local copies, waits for them, and re-layouts  1.41 us
  transfers between devices with their start and end apart: 10, of which 6 were waited for; matrix products, arithmetic and copies ran while one was open for 0% of the time, Pallas kernels for 21%

profile of v3, /device:TPU:1, one launch (start us, length us, event | category | flops | bytes accessed | tf_op | source)
XLA Modules:
  0.0 39.7 jit_solution(14360428241275457839)
XLA Ops:
  0.0 1.1 %shard_map.37 = bf16[192,2,1024]{2,1,0:T(2,128)(2,1)S(1)} custom-call(bf16[384,2,1024]{2,1,0:T(2,128)(2,1)} %doubles.2), custom_call_target="tpu_custom_call" | custom-call | tf_op jit(solution)/shard_map/pallas_call | solution.py:70
  1.1 3.3 %collective-permute-start.4 = (bf16[2,2,1024,1024]{3,2,1,0:T(8,128)(2,1)}, bf16[2,2,1024,1024]{3,2,1,0:T(8,128)(2,1)S(1)}, u32[]{:S(2)}, u32[]{:S(2)}) collective-permute-start(bf16[2,2,1024,1024]{3,2,1,0:T(8,128)(2,1)} %bitcast.3), channel_id=1, source_target_pairs={{0,1},{1,0},{2,3},{3,2},{4,5},{5,4},{6,7},{7,6},{8,9},{9,8},{10,11... | collective-permute-start | bytes 25165832 | tf_op jit(solution)/shard_map/ppermute | solution.py:40
  4.5 1.0 %collective-permute-start.2 = (bf16[192,2,1024]{2,1,0:T(2,128)(2,1)S(1)}, bf16[192,2,1024]{2,1,0:T(2,128)(2,1)S(1)}, u32[]{:S(2)}, u32[]{:S(2)}) collective-permute-start(bf16[192,2,1024]{2,1,0:T(2,128)(2,1)S(1)} %shard_map.37), channel_id=1, source_target_pairs={{0,16},{1,17},{2,18},{3,19},{4,20},{5,21},{6,22},{7,23},{8,24},{9,... | collective-permute-start | bytes 2359304 | tf_op jit(solution)/shard_map/ppermute | solution.py:44
  5.5 1.4 %copy-done = bf16[384,2,1024]{2,1,0:T(2,128)(2,1)S(1)} copy-done((bf16[384,2,1024]{2,1,0:T(2,128)(2,1)S(1)}, bf16[384,2,1024]{2,1,0:T(2,128)(2,1)}, u32[]{:S(2)}) %copy-start) | copy-done | bytes 1572888
  6.9 1.7 %shard_map.38 = (bf16[384,256]{1,0:T(8,128)(2,1)S(1)}, bf16[384,768]{1,0:T(8,128)(2,1)S(1)}) custom-call(bf16[384,2,1024]{2,1,0:T(2,128)(2,1)S(1)} %copy-done), custom_call_target="tpu_custom_call" | custom-call | tf_op jit(solution)/shard_map/pallas_call | solution.py:96
  8.7 1.3 %collective-permute-start = (bf16[384,768]{1,0:T(8,128)(2,1)S(1)}, bf16[384,768]{1,0:T(8,128)(2,1)S(1)}, u32[]{:S(2)}, u32[]{:S(2)}) collective-permute-start(bf16[384,768]{1,0:T(8,128)(2,1)S(1)} %get-tuple-element.19), channel_id=1, source_target_pairs={{6,2},{7,1},{14,10},{15,9},{22,18},{23,17},{30,26},{31,25},{38,34}... | collective-permute-start | bytes 1769480 | tf_op jit(solution)/shard_map/ppermute | solution.py:44
  10.0 2.6 %collective-permute-start.3 = (bf16[384,768]{1,0:T(8,128)(2,1)S(1)}, bf16[384,768]{1,0:T(8,128)(2,1)S(1)}, u32[]{:S(2)}, u32[]{:S(2)}) collective-permute-start(bf16[384,768]{1,0:T(8,128)(2,1)S(1)} %get-tuple-element.19), channel_id=1, source_target_pairs={{0,2},{1,3},{2,4},{3,5},{4,6},{5,7},{8,10},{9,11},{10,12},{11,13},... | collective-permute-start | bytes 1769480 | tf_op jit(solution)/shard_map/ppermute | solution.py:44
  12.6 1.3 %collective-permute-start.1 = (s32[2]{0:T(128)}, s32[2]{0:T(128)S(1)}, u32[]{:S(2)}, u32[]{:S(2)}) collective-permute-start(s32[2]{0:T(128)} %bitcast.5), channel_id=1, source_target_pairs={{0,1},{1,0},{2,3},{3,2},{4,5},{5,4},{6,7},{7,6},{8,9},{9,8},{10,11... | collective-permute-start | bytes 32 | tf_op jit(solution)/shard_map/ppermute | solution.py:40
  13.9 2.2 %shard_map.39.kept = bf16[2,1024,1024]{2,1,0:T(8,128)(2,1)S(1)} custom-call(bf16[2,2,1024,1024]{3,2,1,0:T(8,128)(2,1)} %bitcast.4), custom_call_target="tpu_custom_call" | custom-call | tf_op jit(solution)/shard_map/pallas_call | solution.py:133
  16.1 1.3 %collective-permute-done.1 = s32[2]{0:T(128)S(1)} collective-permute-done((s32[2]{0:T(128)}, s32[2]{0:T(128)S(1)}, u32[]{:S(2)}, u32[]{:S(2)}) %collective-permute-start.1) | collective-permute-done | bytes 40 | tf_op jit(solution)/shard_map/ppermute | solution.py:40
  17.5 0.1 and_select_fusion.parity
  17.6 3.2 %collective-permute-done = bf16[384,768]{1,0:T(8,128)(2,1)S(1)} collective-permute-done((bf16[384,768]{1,0:T(8,128)(2,1)S(1)}, bf16[384,768]{1,0:T(8,128)(2,1)S(1)}, u32[]{:S(2)}, u32[]{:S(2)}) %collective-permute-start) | collective-permute-done | bytes 589856 | tf_op jit(solution)/shard_map/ppermute | solution.py:44
  20.8 2.1 %collective-permute-start.7 = (bf16[384,768]{1,0:T(8,128)(2,1)S(1)}, bf16[384,768]{1,0:T(8,128)(2,1)S(1)}, u32[]{:S(2)}, u32[]{:S(2)}) collective-permute-start(bf16[384,768]{1,0:T(8,128)(2,1)S(1)} %collective-permute-done), channel_id=1, source_target_pairs={{2,8},{1,9},{10,16},{9,17},{18,24},{17,25},{26,0},{25,1},{34,40},{... | collective-permute-start | bytes 1769480 | tf_op jit(solution)/shard_map/ppermute | solution.py:44
  22.8 1.4 %collective-permute-done.3.inside = bf16[384,768]{1,0:T(8,128)(2,1)S(1)} collective-permute-done((bf16[384,768]{1,0:T(8,128)(2,1)S(1)}, bf16[384,768]{1,0:T(8,128)(2,1)S(1)}, u32[]{:S(2)}, u32[]{:S(2)}) %collective-permute-start.3) | collective-permute-done | bytes 589856 | tf_op jit(solution)/shard_map/ppermute | solution.py:44
  24.2 0.9 %collective-permute-done.2.pairs = bf16[192,2,1024]{2,1,0:T(2,128)(2,1)S(1)} collective-permute-done((bf16[192,2,1024]{2,1,0:T(2,128)(2,1)S(1)}, bf16[192,2,1024]{2,1,0:T(2,128)(2,1)S(1)}, u32[]{:S(2)}, u32[]{:S(2)}) %collective-permute-start.2) | collective-permute-done | bytes 786464 | tf_op jit(solution)/shard_map/ppermute | solution.py:44
  25.1 1.7 %shard_map.42.mine = bf16[384,1024]{1,0:T(8,128)(2,1)S(1)} custom-call(bf16[192,2,1024]{2,1,0:T(2,128)(2,1)S(1)} %collective-permute-done.2.pairs), custom_call_target="tpu_custom_call" | custom-call | flops 4600000000 | tf_op jit(solution)/shard_map/pallas_call | solution.py:116
  26.8 2.6 %collective-permute-start.9 = (bf16[384,1024]{1,0:T(8,128)(2,1)S(1)}, bf16[384,1024]{1,0:T(8,128)(2,1)S(1)}, u32[]{:S(2)}, u32[]{:S(2)}) collective-permute-start(bf16[384,1024]{1,0:T(8,128)(2,1)S(1)} %shard_map.42.mine), channel_id=1, source_target_pairs={{0,1},{1,0},{2,3},{3,2},{4,5},{5,4},{6,7},{7,6},{8,9},{9,8},{10,11... | collective-permute-start | bytes 2359304 | tf_op jit(solution)/shard_map/ppermute | solution.py:40
  29.4 1.0 %collective-permute-done.5.refs_0_ = bf16[384,256]{1,0:T(8,128)(2,1)S(1)} collective-permute-done((bf16[384,256]{1,0:T(8,128)(2,1)S(1)}, bf16[384,256]{1,0:T(8,128)(2,1)S(1)}, u32[]{:S(2)}, u32[]{:S(2)}) %collective-permute-start.5) | collective-permute-done | bytes 196640 | tf_op jit(solution)/shard_map/ppermute | solution.py:44
  30.4 0.5 %collective-permute-start.6 = (bf16[384,256]{1,0:T(8,128)(2,1)S(1)}, bf16[384,256]{1,0:T(8,128)(2,1)S(1)}, u32[]{:S(2)}, u32[]{:S(2)}) collective-permute-start(bf16[384,256]{1,0:T(8,128)(2,1)S(1)} %collective-permute-done.5.refs_0_), channel_id=1, source_target_pairs={{0,1},{1,0},{2,3},{3,2},{4,5},{5,4},{6,7},{7,6},{8,9},{9,8},{10,11... | collective-permute-start | bytes 589832 | tf_op jit(solution)/shard_map/ppermute | solution.py:40
  30.9 2.0 %collective-permute-done.7.relayed = bf16[384,768]{1,0:T(8,128)(2,1)S(1)} collective-permute-done((bf16[384,768]{1,0:T(8,128)(2,1)S(1)}, bf16[384,768]{1,0:T(8,128)(2,1)S(1)}, u32[]{:S(2)}, u32[]{:S(2)}) %collective-permute-start.7) | collective-permute-done | bytes 589856 | tf_op jit(solution)/shard_map/ppermute | solution.py:44
  32.9 0.1 shard_map.41.right
  33.0 0.9 %collective-permute-start.8 = (bf16[384,768]{1,0:T(8,128)(2,1)S(1)}, bf16[384,768]{1,0:T(8,128)(2,1)S(1)}, u32[]{:S(2)}, u32[]{:S(2)}) collective-permute-start(bf16[384,768]{1,0:T(8,128)(2,1)S(1)} %shard_map.41.right), channel_id=1, source_target_pairs={{0,1},{1,0},{2,3},{3,2},{4,5},{5,4},{6,7},{7,6},{8,9},{9,8},{10,11... | collective-permute-start | bytes 1769480 | tf_op jit(solution)/shard_map/ppermute | solution.py:40
  34.0 2.4 %shard_map.43.total = f32[384,1024]{1,0:T(8,128)S(1)} custom-call(s32[4]{0:T(128)S(1)} %and_select_fusion.parity, bf16[2,1024,1024]{2,1,0:T(8,128)(2,1)S(1)} %shard_map.39.kept, bf16[2,2,1024,1024]{3,2,1,0:T(8,128)(2,1)S(1)} %collective-permute-done.4.got, bf16[384,1024]{1,0:T(8,128)(2,1)S(1)} %shard_map.42.mine, ...), custom_call_target="tpu_custom_call" | custom-call | tf_op jit(solution)/shard_map/pallas_call | solution.py:193
  36.4 3.3 %shard_map.44 = bf16[384,1024]{1,0:T(8,128)(2,1)} custom-call(s32[4]{0:T(128)S(1)} %and_select_fusion.parity, bf16[2,1024,1024]{2,1,0:T(8,128)(2,1)S(1)} %shard_map.39.kept, bf16[2,2,1024,1024]{3,2,1,0:T(8,128)(2,1)S(1)} %collective-permute-done.4.got, bf16[384,256]{1,0:T(8,128)(2,1)S(1)} %get-tuple-element.26.left, ...), custom_call_target="tpu_custom_call" | custom-call | tf_op jit(solution)/shard_map/pallas_call | solution.py:193
  (9 shorter events, 0.0 us)
Async XLA Ops:
  1.1 23.9 %collective-permute-start.4 = (bf16[2,2,1024,1024]{3,2,1,0:T(8,128)(2,1)}, bf16[2,2,1024,1024]{3,2,1,0:T(8,128)(2,1)S(1)}, u32[]{:S(2)}, u32[]{:S(2)}) collective-permute-start(bf16[2,2,1024,1024]{3,2,1,0:T(8,128)(2,1)} %bitcast.3), channel_id=1, source_target_pairs={{0,1},{1,0},{2,3},{3,2},{4,5},{5,4},{6,7},{7,6},{8,9},{9,8},{10,11... | collective-permute-start | bytes 25165832 | tf_op jit(solution)/shard_map/ppermute | solution.py:40
  4.5 20.6 %collective-permute-start.2 = (bf16[192,2,1024]{2,1,0:T(2,128)(2,1)S(1)}, bf16[192,2,1024]{2,1,0:T(2,128)(2,1)S(1)}, u32[]{:S(2)}, u32[]{:S(2)}) collective-permute-start(bf16[192,2,1024]{2,1,0:T(2,128)(2,1)S(1)} %shard_map.37), channel_id=1, source_target_pairs={{0,16},{1,17},{2,18},{3,19},{4,20},{5,21},{6,22},{7,23},{8,24},{9,... | collective-permute-start | bytes 2359304 | tf_op jit(solution)/shard_map/ppermute | solution.py:44
  5.5 1.4 %copy-start = (bf16[384,2,1024]{2,1,0:T(2,128)(2,1)S(1)}, bf16[384,2,1024]{2,1,0:T(2,128)(2,1)}, u32[]{:S(2)}) copy-start(bf16[384,2,1024]{2,1,0:T(2,128)(2,1)} %doubles.2) | copy-start | bytes 4718596
  8.7 12.1 %collective-permute-start = (bf16[384,768]{1,0:T(8,128)(2,1)S(1)}, bf16[384,768]{1,0:T(8,128)(2,1)S(1)}, u32[]{:S(2)}, u32[]{:S(2)}) collective-permute-start(bf16[384,768]{1,0:T(8,128)(2,1)S(1)} %get-tuple-element.19), channel_id=1, source_target_pairs={{6,2},{7,1},{14,10},{15,9},{22,18},{23,17},{30,26},{31,25},{38,34}... | collective-permute-start | bytes 1769480 | tf_op jit(solution)/shard_map/ppermute | solution.py:44
  10.0 14.3 %collective-permute-start.3 = (bf16[384,768]{1,0:T(8,128)(2,1)S(1)}, bf16[384,768]{1,0:T(8,128)(2,1)S(1)}, u32[]{:S(2)}, u32[]{:S(2)}) collective-permute-start(bf16[384,768]{1,0:T(8,128)(2,1)S(1)} %get-tuple-element.19), channel_id=1, source_target_pairs={{0,2},{1,3},{2,4},{3,5},{4,6},{5,7},{8,10},{9,11},{10,12},{11,13},... | collective-permute-start | bytes 1769480 | tf_op jit(solution)/shard_map/ppermute | solution.py:44
  12.6 4.9 %copy-start.1 = (s32[1,1,2]{2,1,0:T(1,128)S(1)}, s32[1,1,2]{2,1,0:T(1,128)}, u32[]{:S(2)}) copy-start(s32[1,1,2]{2,1,0:T(1,128)} %param.5) | copy-start | bytes 28
  12.6 4.9 %collective-permute-start.1 = (s32[2]{0:T(128)}, s32[2]{0:T(128)S(1)}, u32[]{:S(2)}, u32[]{:S(2)}) collective-permute-start(s32[2]{0:T(128)} %bitcast.5), channel_id=1, source_target_pairs={{0,1},{1,0},{2,3},{3,2},{4,5},{5,4},{6,7},{7,6},{8,9},{9,8},{10,11... | collective-permute-start | bytes 32 | tf_op jit(solution)/shard_map/ppermute | solution.py:40
  17.5 12.9 %collective-permute-start.5 = (bf16[384,256]{1,0:T(8,128)(2,1)S(1)}, bf16[384,256]{1,0:T(8,128)(2,1)S(1)}, u32[]{:S(2)}, u32[]{:S(2)}) collective-permute-start(bf16[384,256]{1,0:T(8,128)(2,1)S(1)} %get-tuple-element.25), channel_id=1, source_target_pairs={{0,2},{1,3},{2,4},{3,5},{4,6},{5,7},{8,10},{9,11},{10,12},{11,13},... | collective-permute-start | bytes 589832 | tf_op jit(solution)/shard_map/ppermute | solution.py:44
  20.8 12.1 %collective-permute-start.7 = (bf16[384,768]{1,0:T(8,128)(2,1)S(1)}, bf16[384,768]{1,0:T(8,128)(2,1)S(1)}, u32[]{:S(2)}, u32[]{:S(2)}) collective-permute-start(bf16[384,768]{1,0:T(8,128)(2,1)S(1)} %collective-permute-done), channel_id=1, source_target_pairs={{2,8},{1,9},{10,16},{9,17},{18,24},{17,25},{26,0},{25,1},{34,40},{... | collective-permute-start | bytes 1769480 | tf_op jit(solution)/shard_map/ppermute | solution.py:44
  26.8 7.2 %collective-permute-start.9 = (bf16[384,1024]{1,0:T(8,128)(2,1)S(1)}, bf16[384,1024]{1,0:T(8,128)(2,1)S(1)}, u32[]{:S(2)}, u32[]{:S(2)}) collective-permute-start(bf16[384,1024]{1,0:T(8,128)(2,1)S(1)} %shard_map.42.mine), channel_id=1, source_target_pairs={{0,1},{1,0},{2,3},{3,2},{4,5},{5,4},{6,7},{7,6},{8,9},{9,8},{10,11... | collective-permute-start | bytes 2359304 | tf_op jit(solution)/shard_map/ppermute | solution.py:40
  30.4 3.6 %collective-permute-start.6 = (bf16[384,256]{1,0:T(8,128)(2,1)S(1)}, bf16[384,256]{1,0:T(8,128)(2,1)S(1)}, u32[]{:S(2)}, u32[]{:S(2)}) collective-permute-start(bf16[384,256]{1,0:T(8,128)(2,1)S(1)} %collective-permute-done.5.refs_0_), channel_id=1, source_target_pairs={{0,1},{1,0},{2,3},{3,2},{4,5},{5,4},{6,7},{7,6},{8,9},{9,8},{10,11... | collective-permute-start | bytes 589832 | tf_op jit(solution)/shard_map/ppermute | solution.py:40
  33.0 3.3 %collective-permute-start.8 = (bf16[384,768]{1,0:T(8,128)(2,1)S(1)}, bf16[384,768]{1,0:T(8,128)(2,1)S(1)}, u32[]{:S(2)}, u32[]{:S(2)}) collective-permute-start(bf16[384,768]{1,0:T(8,128)(2,1)S(1)} %shard_map.41.right), channel_id=1, source_target_pairs={{0,1},{1,0},{2,3},{3,2},{4,5},{5,4},{6,7},{7,6},{8,9},{9,8},{10,11... | collective-permute-start | bytes 1769480 | tf_op jit(solution)/shard_map/ppermute | solution.py:40

commit v4 on v0

v4 whole, which is shorter than its diff:
```python
import functools

import jax
import jax.numpy as jnp
from jax import lax
from jax.experimental import pallas as pl
from jax.experimental.pallas import tpu as pltpu
from jax.sharding import PartitionSpec as P

SWAP = ((0, 1), (1, 0))
CUT = 256
SEPARATE = 2300 * 10**6
HOLD = 4600 * 10**6
TRANSPOSED = (((1,), (1,)), ((), ()))


def device(x, y, core):
    return ((x % 4) * 4 + y % 4) * 2 + core


def chips():
    return [(x, y) for x in range(4) for y in range(4)]


def route(pairs):
    return tuple((device(*a), device(*b)) for a, b in pairs)


ACROSS = route(((x, y, c), (x + 2, y, c)) for x, y in chips() for c in (0, 1))
INSIDE = route(((x, y, c), (x, y + 1, c)) for x, y in chips() for c in (0, 1) if y < 3)
WRAP = route(((x, 3, c), (x + 1, 0, c)) for x in range(4) for c in (0, 1))
RELAY_ROW = {0: 1, 1: 0}
RELAY_Y = route(((x, 3, c), (x, RELAY_ROW[c], c)) for x in range(4) for c in (0, 1))
RELAY_X = route(((x, RELAY_ROW[c], c), (x + 1, 0, c)) for x in range(4) for c in (0, 1))


def swap(value):
    return lax.ppermute(value, "stream", SWAP)


def send(value, pairs):
    return lax.ppermute(value, ("vir", "stream"), pairs)


VMEM = pl.BlockSpec(memory_space=pltpu.VMEM)
SMEM = pl.BlockSpec(memory_space=pltpu.SMEM)
ANYWHERE = pl.BlockSpec(memory_space=pl.ANY)


def params(mebibytes):
    return pltpu.CompilerParams(vmem_limit_bytes=mebibytes * 2**20)


def in_hbm(value):
    return pltpu.with_memory_space_constraint(value, pltpu.HBM)


def cut_kernel(doubles, out, arrived):
    rows = out.shape[0]
    core = lax.axis_index("stream")
    copy = pltpu.make_async_copy(doubles.at[pl.ds(core * rows, rows)], out, arrived)
    copy.start()
    copy.wait()


def cut_rows(doubles):
    shape = (doubles.shape[0] // 2, *doubles.shape[1:])
    return pl.pallas_call(
        cut_kernel,
        out_shape=jax.ShapeDtypeStruct(shape, doubles.dtype),
        in_specs=[pl.BlockSpec(memory_space=pltpu.HBM)],
        out_specs=VMEM,
        scratch_shapes=[pltpu.SemaphoreType.DMA],
        compiler_params=params(1),
    )(in_hbm(doubles))


def separate_kernel(pairs, out):
    rows = pairs.shape[0]
    out[:rows] = pairs[:, 0, :]
    out[rows:] = pairs[:, 1, :]


def separate_wrap_kernel(pairs, left, right):
    rows = pairs.shape[0]

    @pl.when(lax.axis_index("vir") % 4 == 3)
    def _():
        for pair in (0, 1):
            place = pl.ds(pair * rows, rows)
            left[place] = pairs[:, pair, :CUT]
            right[place] = pairs[:, pair, CUT:]


def separate_next_kernel(inside, direct, relayed, out):
    wrapped = lax.axis_index("vir") % 4 == 0

    @pl.when(jnp.logical_not(wrapped))
    def _():
        separate_kernel(inside, out)

    @pl.when(wrapped)
    def _():
        out[:, :CUT] = direct[...]
        out[:, CUT:] = relayed[...]


def separate(kernel, flops, widths, *operands):
    rows, count, _ = operands[0].shape
    return pl.pallas_call(
        kernel,
        out_shape=[
            jax.ShapeDtypeStruct((rows * count, width), operands[0].dtype) for width in widths
        ],
        in_specs=[VMEM] * len(operands),
        out_specs=[VMEM] * len(widths),
        cost_estimate=pl.CostEstimate(flops=flops, bytes_accessed=0, transcendentals=0),
        compiler_params=params(4),
    )(*operands)


def keep_kernel(blocks, out, arrived):
    copy = pltpu.make_async_copy(blocks.at[lax.axis_index("stream")], out, arrived)
    copy.start()
    copy.wait()


def keep(blocks):
    return pl.pallas_call(
        keep_kernel,
        out_shape=jax.ShapeDtypeStruct(blocks.shape[1:], blocks.dtype),
        in_specs=[pl.BlockSpec(memory_space=pltpu.HBM)],
        out_specs=VMEM,
        scratch_shapes=[pltpu.SemaphoreType.DMA],
        compiler_params=params(1),
    )(in_hbm(blocks))


def hold_kernel(*refs):
    pass


def hold(*values, flops):
    return pl.pallas_call(
        hold_kernel,
        out_shape=[jax.ShapeDtypeStruct(value.shape, value.dtype) for value in values],
        in_specs=[ANYWHERE] * len(values),
        out_specs=[ANYWHERE] * len(values),
        input_output_aliases={i: i for i in range(len(values))},
        cost_estimate=pl.CostEstimate(flops=flops, bytes_accessed=0, transcendentals=0),
        compiler_params=params(1),
    )(*values)


def multiply(picked, block):
    return lax.dot_general(picked, block, TRANSPOSED, preferred_element_type=jnp.float32)


def sum_kernel(slot, has_total, parity, kept, got, mine, other, *refs):
    out = refs[-1]
    core = lax.axis_index("stream")
    rows = mine.shape[0] // 2
    total = refs[0][...] if has_total else 0
    for holder, block in ((0, kept[slot]), (1, got[core, slot])):
        second = parity[holder * 2 + slot] == 1
        halves = [jnp.where(second, half[rows:], half[:rows]) for half in (mine, other)]
        upper = jnp.where(core == 0, halves[0], halves[1])
        lower = jnp.where(core == 0, halves[1], halves[0])
        total = total + multiply(jnp.concatenate([upper, lower], 0), block)
    out[...] = total.astype(out.dtype)


def add_slot(slot, dtype, parity, *operands):
    return pl.pallas_call(
        functools.partial(sum_kernel, slot, len(operands) == 5),
        out_shape=jax.ShapeDtypeStruct(operands[2].shape, dtype),
        in_specs=[SMEM] + [VMEM] * len(operands),
        out_specs=VMEM,
        cost_estimate=pl.CostEstimate(flops=0, bytes_accessed=0, transcendentals=0),
        compiler_params=params(12),
    )(parity, *operands)


def on_device(doubles, integrals, tiles):
    rows = cut_rows(doubles)
    across = send(rows, ACROSS)
    inside = send(rows, INSIDE)
    left, right = separate(separate_wrap_kernel, 0, (CUT, 1024 - CUT), rows)
    relayed = send(send(right, RELAY_Y), RELAY_X)
    direct = send(left, WRAP)

    blocks, _ = lax.optimization_barrier((integrals[0, 0], rows))
    got, tiles = lax.optimization_barrier((swap(blocks), tiles))
    kept = keep(blocks)
    used = tiles[0, 0]
    parity = jnp.concatenate([used, swap(used)]) % 2
    (across,) = separate(separate_kernel, SEPARATE, (1024,), across)
    across, inside, kept, got, parity = lax.optimization_barrier(
        (across, inside, kept, got, parity)
    )
    total = add_slot(1, jnp.float32, parity, kept, got, across, swap(across))
    (direct,) = hold(direct, flops=HOLD)
    (first,) = separate(separate_next_kernel, 0, (1024,), inside, direct, relayed)
    out = add_slot(0, jnp.bfloat16, parity, kept, got, first, swap(first), total)
    return out[:, None]


def solution(mesh):
    placed = (
        P("occ", "vir", None),
        P("vir", "stream", None, None, None, None),
        P("vir", "stream", None),
    )
    return jax.shard_map(
        on_device,
        mesh=mesh,
        in_specs=placed,
        out_specs=P("occ", ("vir", "stream"), None),
        check_vma=False,
    )
```

time: 211 us -> 37.7 us (0.18)
  waiting for transfers between devices: 163 us -> 13 us
  local copies, waits for them, and re-layouts: 13.5 us -> 0.01 us
  starting transfers between devices: 0.01 us -> 13.4 us
  between operations: 13.4 us -> 0.12 us
  blocking collectives: 12.8 us -> 0 us
  Pallas kernels: 0 us -> 10.8 us
  matrix products: 8.54 us -> 0 us
    all_gather x1 -> x0, waiting for transfers between devices: 163 us -> none  [on_device(): whole = lax.all_gather(doubles, 'vir', axis=1, tiled=True)]
    ppermute x0 -> x9, starting transfers between devices: none -> 13.4 us  [the longest x5 8.21 us: send(): return lax.ppermute(value, ('vir', 'stream'), pairs)]
    ppermute x0 -> x9, waiting for transfers between devices: none -> 13 us  [the longest x5 12.2 us: send(): return lax.ppermute(value, ('vir', 'stream'), pairs)]
    psum x1 -> x0, blocking collectives: 12.8 us -> none  [on_device(): summed = lax.psum(partial_value, 'stream')]
    pallas_call x0 -> x8, Pallas kernels: none -> 10.8 us  [the longest x2 5.64 us: add_slot(): pl.pallas_call(functools.partial(sum_kernel, slot, len(operands) == 5), o...]
    gather x1 -> x0, local copies, waits for them, and re-layouts: 8.8 us -> none  [on_device(): picked = jnp.take(whole, used, axis=1)]
    dot_general x1 -> x0, matrix products: 8.54 us -> none  [on_device(): jnp.einsum('osq,aspq->oap', picked, integrals[0, 0], preferred_element_ty...]
    unnamed x3 -> x2, local copies, waits for them, and re-layouts: 3.71 us -> 0.01 us
  transfers between devices with their start and end apart: 1 -> 9, of which waited for: 1 -> 5; matrix products, arithmetic and copies ran while one was open for 0% -> 0% of each run, Pallas kernels for 0% -> 17%
where the time goes in v4:
time: 37.7 us; the launch traced here: 37.4 us
  starting transfers between devices  13.4 us (36%)
  waiting for transfers between devices  13 us (34%)
  Pallas kernels  10.8 us (29%)
    ppermute x5, waiting for transfers between devices, send(): return lax.ppermute(value, ('vir', 'stream'), pairs)  12.2 us
    ppermute x5, starting transfers between devices, send(): return lax.ppermute(value, ('vir', 'stream'), pairs)  8.21 us
    pallas_call x2, Pallas kernels, add_slot(): pl.pallas_call(functools.partial(sum_kernel, slot, len(operands) == 5), o...  5.64 us
    ppermute x4, starting transfers between devices, swap(): return lax.ppermute(value, 'stream', SWAP)  5.22 us
    pallas_call x1, Pallas kernels, keep(): pl.pallas_call(keep_kernel, out_shape=jax.ShapeDtypeStruct(blocks.shape[1...  2.2 us
    pallas_call x3, Pallas kernels, separate(): pl.pallas_call(kernel, out_shape=[jax.ShapeDtypeStruct((rows * count, wid...  1.79 us
    pallas_call x1, Pallas kernels, cut_rows(): pl.pallas_call(cut_kernel, out_shape=jax.ShapeDtypeStruct(shape, doubles....  1.14 us
    ppermute x4, waiting for transfers between devices, swap(): return lax.ppermute(value, 'stream', SWAP)  0.83 us
  transfers between devices with their start and end apart: 9, of which 5 were waited for; matrix products, arithmetic and copies ran while one was open for 0% of the time, Pallas kernels for 17%

profile of v4, /device:TPU:1, one launch (start us, length us, event | category | flops | bytes accessed | tf_op | source)
XLA Modules:
  0.0 37.4 jit_solution(3949746392199032366)
XLA Ops:
  0.0 1.1 %shard_map.37.pairs = bf16[192,2,1024]{2,1,0:T(2,128)(2,1)S(1)} custom-call(bf16[384,2,1024]{2,1,0:T(2,128)(2,1)} %doubles.1), custom_call_target="tpu_custom_call" | custom-call | tf_op jit(solution)/shard_map/pallas_call | solution.py:68
  1.1 3.3 %collective-permute-start.2 = (bf16[2,2,1024,1024]{3,2,1,0:T(8,128)(2,1)}, bf16[2,2,1024,1024]{3,2,1,0:T(8,128)(2,1)S(1)}, u32[]{:S(2)}, u32[]{:S(2)}) collective-permute-start(bf16[2,2,1024,1024]{3,2,1,0:T(8,128)(2,1)} %bitcast.3), channel_id=1, source_target_pairs={{0,1},{1,0},{2,3},{3,2},{4,5},{5,4},{6,7},{7,6},{8,9},{9,8},{10,11... | collective-permute-start | bytes 25165832 | tf_op jit(solution)/shard_map/ppermute | solution.py:38
  4.5 1.0 %collective-permute-start = (bf16[192,2,1024]{2,1,0:T(2,128)(2,1)S(1)}, bf16[192,2,1024]{2,1,0:T(2,128)(2,1)S(1)}, u32[]{:S(2)}, u32[]{:S(2)}) collective-permute-start(bf16[192,2,1024]{2,1,0:T(2,128)(2,1)S(1)} %shard_map.37.pairs), channel_id=1, source_target_pairs={{0,16},{1,17},{2,18},{3,19},{4,20},{5,21},{6,22},{7,23},{8,24},{9,... | collective-permute-start | bytes 2359304 | tf_op jit(solution)/shard_map/ppermute | solution.py:42
  5.5 1.3 %collective-permute-start.5 = (bf16[384,768]{1,0:T(8,128)(2,1)S(1)}, bf16[384,768]{1,0:T(8,128)(2,1)S(1)}, u32[]{:S(2)}, u32[]{:S(2)}) collective-permute-start(bf16[384,768]{1,0:T(8,128)(2,1)S(1)} %get-tuple-element.23), channel_id=1, source_target_pairs={{6,2},{7,1},{14,10},{15,9},{22,18},{23,17},{30,26},{31,25},{38,34}... | collective-permute-start | bytes 1769480 | tf_op jit(solution)/shard_map/ppermute | solution.py:42
  6.8 2.7 %collective-permute-start.1 = (bf16[192,2,1024]{2,1,0:T(2,128)(2,1)S(1)}, bf16[192,2,1024]{2,1,0:T(2,128)(2,1)S(1)}, u32[]{:S(2)}, u32[]{:S(2)}) collective-permute-start(bf16[192,2,1024]{2,1,0:T(2,128)(2,1)S(1)} %shard_map.37.pairs), channel_id=1, source_target_pairs={{0,2},{1,3},{2,4},{3,5},{4,6},{5,7},{8,10},{9,11},{10,12},{11,13},... | collective-permute-start | bytes 2359304 | tf_op jit(solution)/shard_map/ppermute | solution.py:42
  9.5 1.3 %collective-permute-start.4 = (bf16[384,256]{1,0:T(8,128)(2,1)S(1)}, bf16[384,256]{1,0:T(8,128)(2,1)S(1)}, u32[]{:S(2)}, u32[]{:S(2)}) collective-permute-start(bf16[384,256]{1,0:T(8,128)(2,1)S(1)} %get-tuple-element.22), channel_id=1, source_target_pairs={{6,8},{7,9},{14,16},{15,17},{22,24},{23,25},{30,0},{31,1},{38,40},... | collective-permute-start | bytes 589832 | tf_op jit(solution)/shard_map/ppermute | solution.py:42
  10.8 2.2 %shard_map.39.kept = bf16[2,1024,1024]{2,1,0:T(8,128)(2,1)S(1)} custom-call(bf16[2,2,1024,1024]{3,2,1,0:T(8,128)(2,1)} %bitcast.4), custom_call_target="tpu_custom_call" | custom-call | tf_op jit(solution)/shard_map/pallas_call | solution.py:129
  13.0 0.0 copy-start
  13.0 5.9 %collective-permute-done.5 = bf16[384,768]{1,0:T(8,128)(2,1)S(1)} collective-permute-done((bf16[384,768]{1,0:T(8,128)(2,1)S(1)}, bf16[384,768]{1,0:T(8,128)(2,1)S(1)}, u32[]{:S(2)}, u32[]{:S(2)}) %collective-permute-start.5) | collective-permute-done | bytes 589856 | tf_op jit(solution)/shard_map/ppermute | solution.py:42
  18.9 2.0 %collective-permute-start.6 = (bf16[384,768]{1,0:T(8,128)(2,1)S(1)}, bf16[384,768]{1,0:T(8,128)(2,1)S(1)}, u32[]{:S(2)}, u32[]{:S(2)}) collective-permute-start(bf16[384,768]{1,0:T(8,128)(2,1)S(1)} %collective-permute-done.5), channel_id=1, source_target_pairs={{2,8},{1,9},{10,16},{9,17},{18,24},{17,25},{26,0},{25,1},{34,40},{... | collective-permute-start | bytes 1769480 | tf_op jit(solution)/shard_map/ppermute | solution.py:42
  20.9 4.2 %collective-permute-done.pairs = bf16[192,2,1024]{2,1,0:T(2,128)(2,1)S(1)} collective-permute-done((bf16[192,2,1024]{2,1,0:T(2,128)(2,1)S(1)}, bf16[192,2,1024]{2,1,0:T(2,128)(2,1)S(1)}, u32[]{:S(2)}, u32[]{:S(2)}) %collective-permute-start) | collective-permute-done | bytes 786464 | tf_op jit(solution)/shard_map/ppermute | solution.py:42
  25.1 1.7 %shard_map.38.mine = bf16[384,1024]{1,0:T(8,128)(2,1)S(1)} custom-call(bf16[192,2,1024]{2,1,0:T(2,128)(2,1)S(1)} %collective-permute-done.pairs), custom_call_target="tpu_custom_call" | custom-call | flops 2300000000 | tf_op jit(solution)/shard_map/pallas_call | solution.py:110
  26.8 1.4 %collective-permute-start.3 = (s32[2]{0:T(128)S(1)}, s32[2]{0:T(128)S(1)}, u32[]{:S(2)}, u32[]{:S(2)}) collective-permute-start(s32[2]{0:T(128)S(1)} %bitcast.5), channel_id=1, source_target_pairs={{0,1},{1,0},{2,3},{3,2},{4,5},{5,4},{6,7},{7,6},{8,9},{9,8},{10,11... | collective-permute-start | bytes 32 | tf_op jit(solution)/shard_map/ppermute | solution.py:38
  28.3 0.8 %collective-permute-done.3 = s32[2]{0:T(128)S(1)} collective-permute-done((s32[2]{0:T(128)S(1)}, s32[2]{0:T(128)S(1)}, u32[]{:S(2)}, u32[]{:S(2)}) %collective-permute-start.3) | collective-permute-done | bytes 40 | tf_op jit(solution)/shard_map/ppermute | solution.py:38
  29.1 0.1 and_select_fusion.parity
  29.2 0.4 collective-permute-start.8
  29.5 0.9 %collective-permute-done.4.refs_0_ = bf16[384,256]{1,0:T(8,128)(2,1)S(1)} collective-permute-done((bf16[384,256]{1,0:T(8,128)(2,1)S(1)}, bf16[384,256]{1,0:T(8,128)(2,1)S(1)}, u32[]{:S(2)}, u32[]{:S(2)}) %collective-permute-start.4) | collective-permute-done | bytes 196640 | tf_op jit(solution)/shard_map/ppermute | solution.py:42
  30.4 1.2 %collective-permute-done.6.relayed = bf16[384,768]{1,0:T(8,128)(2,1)S(1)} collective-permute-done((bf16[384,768]{1,0:T(8,128)(2,1)S(1)}, bf16[384,768]{1,0:T(8,128)(2,1)S(1)}, u32[]{:S(2)}, u32[]{:S(2)}) %collective-permute-start.6) | collective-permute-done | bytes 589856 | tf_op jit(solution)/shard_map/ppermute | solution.py:42
  31.6 0.1 shard_map.42.mine
  31.7 0.1 collective-permute-start.7
  31.8 0.0 collective-permute-done.8.other
  31.8 2.4 %shard_map.43.refs_0_ = f32[384,1024]{1,0:T(8,128)S(1)} custom-call(s32[4]{0:T(128)S(1)} %and_select_fusion.parity, bf16[2,1024,1024]{2,1,0:T(8,128)(2,1)S(1)} %shard_map.39.kept, bf16[2,2,1024,1024]{3,2,1,0:T(8,128)(2,1)S(1)} %collective-permute-done.2.got, bf16[384,1024]{1,0:T(8,128)(2,1)S(1)} %shard_map.38.mine, ...), custom_call_target="tpu_custom_call" | custom-call | tf_op jit(solution)/shard_map/pallas_call | solution.py:174
  34.2 0.0 collective-permute-done.7.other
  34.2 3.3 %shard_map.44 = bf16[384,1024]{1,0:T(8,128)(2,1)} custom-call(s32[4]{0:T(128)S(1)} %and_select_fusion.parity, bf16[2,1024,1024]{2,1,0:T(8,128)(2,1)S(1)} %shard_map.39.kept, bf16[2,2,1024,1024]{3,2,1,0:T(8,128)(2,1)S(1)} %collective-permute-done.2.got, bf16[384,1024]{1,0:T(8,128)(2,1)S(1)} %shard_map.42.mine, ...), custom_call_target="tpu_custom_call" | custom-call | tf_op jit(solution)/shard_map/pallas_call | solution.py:174
  (5 shorter events, 0.0 us)
Async XLA Ops:
  1.1 25.7 %collective-permute-start.2 = (bf16[2,2,1024,1024]{3,2,1,0:T(8,128)(2,1)}, bf16[2,2,1024,1024]{3,2,1,0:T(8,128)(2,1)S(1)}, u32[]{:S(2)}, u32[]{:S(2)}) collective-permute-start(bf16[2,2,1024,1024]{3,2,1,0:T(8,128)(2,1)} %bitcast.3), channel_id=1, source_target_pairs={{0,1},{1,0},{2,3},{3,2},{4,5},{5,4},{6,7},{7,6},{8,9},{9,8},{10,11... | collective-permute-start | bytes 25165832 | tf_op jit(solution)/shard_map/ppermute | solution.py:38
  4.5 20.6 %collective-permute-start = (bf16[192,2,1024]{2,1,0:T(2,128)(2,1)S(1)}, bf16[192,2,1024]{2,1,0:T(2,128)(2,1)S(1)}, u32[]{:S(2)}, u32[]{:S(2)}) collective-permute-start(bf16[192,2,1024]{2,1,0:T(2,128)(2,1)S(1)} %shard_map.37.pairs), channel_id=1, source_target_pairs={{0,16},{1,17},{2,18},{3,19},{4,20},{5,21},{6,22},{7,23},{8,24},{9,... | collective-permute-start | bytes 2359304 | tf_op jit(solution)/shard_map/ppermute | solution.py:42
  5.5 13.4 %collective-permute-start.5 = (bf16[384,768]{1,0:T(8,128)(2,1)S(1)}, bf16[384,768]{1,0:T(8,128)(2,1)S(1)}, u32[]{:S(2)}, u32[]{:S(2)}) collective-permute-start(bf16[384,768]{1,0:T(8,128)(2,1)S(1)} %get-tuple-element.23), channel_id=1, source_target_pairs={{6,2},{7,1},{14,10},{15,9},{22,18},{23,17},{30,26},{31,25},{38,34}... | collective-permute-start | bytes 1769480 | tf_op jit(solution)/shard_map/ppermute | solution.py:42
  6.8 22.4 %collective-permute-start.1 = (bf16[192,2,1024]{2,1,0:T(2,128)(2,1)S(1)}, bf16[192,2,1024]{2,1,0:T(2,128)(2,1)S(1)}, u32[]{:S(2)}, u32[]{:S(2)}) collective-permute-start(bf16[192,2,1024]{2,1,0:T(2,128)(2,1)S(1)} %shard_map.37.pairs), channel_id=1, source_target_pairs={{0,2},{1,3},{2,4},{3,5},{4,6},{5,7},{8,10},{9,11},{10,12},{11,13},... | collective-permute-start | bytes 2359304 | tf_op jit(solution)/shard_map/ppermute | solution.py:42
  9.5 20.9 %collective-permute-start.4 = (bf16[384,256]{1,0:T(8,128)(2,1)S(1)}, bf16[384,256]{1,0:T(8,128)(2,1)S(1)}, u32[]{:S(2)}, u32[]{:S(2)}) collective-permute-start(bf16[384,256]{1,0:T(8,128)(2,1)S(1)} %get-tuple-element.22), channel_id=1, source_target_pairs={{6,8},{7,9},{14,16},{15,17},{22,24},{23,25},{30,0},{31,1},{38,40},... | collective-permute-start | bytes 589832 | tf_op jit(solution)/shard_map/ppermute | solution.py:42
  13.0 13.9 %copy-start = (s32[1,1,2]{2,1,0:T(1,128)S(1)}, s32[1,1,2]{2,1,0:T(1,128)}, u32[]{:S(2)}) copy-start(s32[1,1,2]{2,1,0:T(1,128)} %param.5) | copy-start | bytes 28
  18.9 12.7 %collective-permute-start.6 = (bf16[384,768]{1,0:T(8,128)(2,1)S(1)}, bf16[384,768]{1,0:T(8,128)(2,1)S(1)}, u32[]{:S(2)}, u32[]{:S(2)}) collective-permute-start(bf16[384,768]{1,0:T(8,128)(2,1)S(1)} %collective-permute-done.5), channel_id=1, source_target_pairs={{2,8},{1,9},{10,16},{9,17},{18,24},{17,25},{26,0},{25,1},{34,40},{... | collective-permute-start | bytes 1769480 | tf_op jit(solution)/shard_map/ppermute | solution.py:42
  26.8 2.2 %collective-permute-start.3 = (s32[2]{0:T(128)S(1)}, s32[2]{0:T(128)S(1)}, u32[]{:S(2)}, u32[]{:S(2)}) collective-permute-start(s32[2]{0:T(128)S(1)} %bitcast.5), channel_id=1, source_target_pairs={{0,1},{1,0},{2,3},{3,2},{4,5},{5,4},{6,7},{7,6},{8,9},{9,8},{10,11... | collective-permute-start | bytes 32 | tf_op jit(solution)/shard_map/ppermute | solution.py:38
  29.2 2.6 %collective-permute-start.8 = (bf16[384,1024]{1,0:T(8,128)(2,1)S(1)}, bf16[384,1024]{1,0:T(8,128)(2,1)S(1)}, u32[]{:S(2)}, u32[]{:S(2)}) collective-permute-start(bf16[384,1024]{1,0:T(8,128)(2,1)S(1)} %shard_map.38.mine), channel_id=1, source_target_pairs={{0,1},{1,0},{2,3},{3,2},{4,5},{5,4},{6,7},{7,6},{8,9},{9,8},{10,11... | collective-permute-start | bytes 2359304 | tf_op jit(solution)/shard_map/ppermute | solution.py:38
  31.7 2.5 %collective-permute-start.7 = (bf16[384,1024]{1,0:T(8,128)(2,1)S(1)}, bf16[384,1024]{1,0:T(8,128)(2,1)S(1)}, u32[]{:S(2)}, u32[]{:S(2)}) collective-permute-start(bf16[384,1024]{1,0:T(8,128)(2,1)S(1)} %shard_map.42.mine), channel_id=1, source_target_pairs={{0,1},{1,0},{2,3},{3,2},{4,5},{5,4},{6,7},{7,6},{8,9},{9,8},{10,11... | collective-permute-start | bytes 2359304 | tf_op jit(solution)/shard_map/ppermute | solution.py:38

commit v5 on v4

--- a/solution.py
+++ b/solution.py
@@ -81,15 +81,13 @@
     out[rows:] = pairs[:, 1, :]
 
 
-def separate_wrap_kernel(pairs, left, right):
-    rows = pairs.shape[0]
+def separate_wrap_kernel(low, pairs, out):
+    rows, width = pairs.shape[0], out.shape[1]
 
     @pl.when(lax.axis_index("vir") % 4 == 3)
     def _():
         for pair in (0, 1):
-            place = pl.ds(pair * rows, rows)
-            left[place] = pairs[:, pair, :CUT]
-            right[place] = pairs[:, pair, CUT:]
+            out[pl.ds(pair * rows, rows)] = pairs[:, pair, low : low + width]
 
 
 def separate_next_kernel(inside, direct, relayed, out):
@@ -156,26 +154,46 @@
     return lax.dot_general(picked, block, TRANSPOSED, preferred_element_type=jnp.float32)
 
 
-def sum_kernel(slot, has_total, parity, kept, got, mine, other, *refs):
-    out = refs[-1]
+def picks(slot, parity, mine, other):
     core = lax.axis_index("stream")
     rows = mine.shape[0] // 2
-    total = refs[0][...] if has_total else 0
-    for holder, block in ((0, kept[slot]), (1, got[core, slot])):
+    for holder in (0, 1):
         second = parity[holder * 2 + slot] == 1
         halves = [jnp.where(second, half[rows:], half[:rows]) for half in (mine, other)]
         upper = jnp.where(core == 0, halves[0], halves[1])
         lower = jnp.where(core == 0, halves[1], halves[0])
-        total = total + multiply(jnp.concatenate([upper, lower], 0), block)
-    out[...] = total.astype(out.dtype)
-
-
-def add_slot(slot, dtype, parity, *operands):
-    return pl.pallas_call(
-        functools.partial(sum_kernel, slot, len(operands) == 5),
+        yield jnp.concatenate([upper, lower], 0)
+
+
+def across_kernel(parity, kept, got, mine, other, out):
+    first, second = picks(1, parity, mine, other)
+    core = lax.axis_index("stream")
+    out[...] = multiply(first, kept[1]) + multiply(second, got[core, 1])
+
+
+def next_kernel(parity, kept, got, mine, other, total, out, ready, sent):
+    first, second = picks(0, parity, mine, other)
+    core = lax.axis_index("stream")
+    width = total.shape[1] // 2
+    copies = []
+    for i in (0, 1):
+        place = pl.ds(i * width, width)
+        result = total[:, place] + multiply(first, kept[0, place])
+        result = result + multiply(second, got[core, 0, place])
+        ready[:, place] = result.astype(ready.dtype)
+        copies.append(pltpu.make_async_copy(ready.at[:, place], out.at[:, place], sent.at[i]))
+        copies[i].start()
+    for copy in copies:
+        copy.wait()
+
+
+def sum_call(kernel, dtype, out_spec, scratch, parity, *operands):
+    return pl.pallas_call(
+        kernel,
         out_shape=jax.ShapeDtypeStruct(operands[2].shape, dtype),
         in_specs=[SMEM] + [VMEM] * len(operands),
-        out_specs=VMEM,
+        out_specs=out_spec,
+        scratch_shapes=scratch,
         cost_estimate=pl.CostEstimate(flops=0, bytes_accessed=0, transcendentals=0),
         compiler_params=params(12),
     )(parity, *operands)
@@ -185,7 +203,8 @@
     rows = cut_rows(doubles)
     across = send(rows, ACROSS)
     inside = send(rows, INSIDE)
-    left, right = separate(separate_wrap_kernel, 0, (CUT, 1024 - CUT), rows)
+    (right,) = separate(functools.partial(separate_wrap_kernel, CUT), 0, (1024 - CUT,), rows)
+    (left,) = separate(functools.partial(separate_wrap_kernel, 0), 0, (CUT,), rows)
     relayed = send(send(right, RELAY_Y), RELAY_X)
     direct = send(left, WRAP)
 
@@ -195,13 +214,25 @@
     used = tiles[0, 0]
     parity = jnp.concatenate([used, swap(used)]) % 2
     (across,) = separate(separate_kernel, SEPARATE, (1024,), across)
-    across, inside, kept, got, parity = lax.optimization_barrier(
-        (across, inside, kept, got, parity)
-    )
-    total = add_slot(1, jnp.float32, parity, kept, got, across, swap(across))
+    across, kept, got, parity = lax.optimization_barrier((across, kept, got, parity))
+    total = sum_call(
+        across_kernel, jnp.float32, VMEM, [], parity, kept, got, across, swap(across)
+    )
     (direct,) = hold(direct, flops=HOLD)
     (first,) = separate(separate_next_kernel, 0, (1024,), inside, direct, relayed)
-    out = add_slot(0, jnp.bfloat16, parity, kept, got, first, swap(first), total)
+    scratch = [pltpu.VMEM(first.shape, jnp.bfloat16), pltpu.SemaphoreType.DMA((2,))]
+    out = sum_call(
+        next_kernel,
+        jnp.bfloat16,
+        ANYWHERE,
+        scratch,
+        parity,
+        kept,
+        got,
+        first,
+        swap(first),
+        total,
+    )
     return out[:, None]
 
 

time: 37.7 us -> 37.5 us (level)
    pallas_call x3 -> x4, Pallas kernels: 1.79 us -> 1.81 us  [separate(): pl.pallas_call(kernel, out_shape=[jax.ShapeDtypeStruct((rows * count, wid...]
where the time goes in v5:
time: 37.5 us; the launch traced here: 37.3 us
  starting transfers between devices  13.4 us (36%)
  waiting for transfers between devices  13 us (35%)
  Pallas kernels  10.7 us (29%)
    ppermute x5, waiting for transfers between devices, send(): return lax.ppermute(value, ('vir', 'stream'), pairs)  12.2 us
    ppermute x5, starting transfers between devices, send(): return lax.ppermute(value, ('vir', 'stream'), pairs)  8.21 us
    pallas_call x2, Pallas kernels, sum_call(): pl.pallas_call(kernel, out_shape=jax.ShapeDtypeStruct(operands[2].shape,...  5.53 us
    ppermute x4, starting transfers between devices, swap(): return lax.ppermute(value, 'stream', SWAP)  5.17 us
    pallas_call x1, Pallas kernels, keep(): pl.pallas_call(keep_kernel, out_shape=jax.ShapeDtypeStruct(blocks.shape[1...  2.2 us
    pallas_call x4, Pallas kernels, separate(): pl.pallas_call(kernel, out_shape=[jax.ShapeDtypeStruct((rows * count, wid...  1.81 us
    pallas_call x1, Pallas kernels, cut_rows(): pl.pallas_call(cut_kernel, out_shape=jax.ShapeDtypeStruct(shape, doubles....  1.14 us
    ppermute x4, waiting for transfers between devices, swap(): return lax.ppermute(value, 'stream', SWAP)  0.83 us
  transfers between devices with their start and end apart: 9, of which 5 were waited for; matrix products, arithmetic and copies ran while one was open for 0% of the time, Pallas kernels for 17%

profile of v5, /device:TPU:1, one launch (start us, length us, event | category | flops | bytes accessed | tf_op | source)
XLA Modules:
  0.0 37.3 jit_solution(3406318953687183435)
XLA Ops:
  0.0 1.1 %shard_map.37.pairs = bf16[192,2,1024]{2,1,0:T(2,128)(2,1)S(1)} custom-call(bf16[384,2,1024]{2,1,0:T(2,128)(2,1)} %doubles.1), custom_call_target="tpu_custom_call" | custom-call | tf_op jit(solution)/shard_map/pallas_call | solution.py:68
  1.1 3.3 %collective-permute-start.1 = (bf16[2,2,1024,1024]{3,2,1,0:T(8,128)(2,1)}, bf16[2,2,1024,1024]{3,2,1,0:T(8,128)(2,1)S(1)}, u32[]{:S(2)}, u32[]{:S(2)}) collective-permute-start(bf16[2,2,1024,1024]{3,2,1,0:T(8,128)(2,1)} %bitcast.3), channel_id=1, source_target_pairs={{0,1},{1,0},{2,3},{3,2},{4,5},{5,4},{6,7},{7,6},{8,9},{9,8},{10,11... | collective-permute-start | bytes 25165832 | tf_op jit(solution)/shard_map/ppermute | solution.py:38
  4.5 1.0 %collective-permute-start = (bf16[192,2,1024]{2,1,0:T(2,128)(2,1)S(1)}, bf16[192,2,1024]{2,1,0:T(2,128)(2,1)S(1)}, u32[]{:S(2)}, u32[]{:S(2)}) collective-permute-start(bf16[192,2,1024]{2,1,0:T(2,128)(2,1)S(1)} %shard_map.37.pairs), channel_id=1, source_target_pairs={{0,16},{1,17},{2,18},{3,19},{4,20},{5,21},{6,22},{7,23},{8,24},{9,... | collective-permute-start | bytes 2359304 | tf_op jit(solution)/shard_map/ppermute | solution.py:42
  5.5 1.3 %collective-permute-start.5 = (bf16[384,768]{1,0:T(8,128)(2,1)S(1)}, bf16[384,768]{1,0:T(8,128)(2,1)S(1)}, u32[]{:S(2)}, u32[]{:S(2)}) collective-permute-start(bf16[384,768]{1,0:T(8,128)(2,1)S(1)} %shard_map.42), channel_id=1, source_target_pairs={{6,2},{7,1},{14,10},{15,9},{22,18},{23,17},{30,26},{31,25},{38,34}... | collective-permute-start | bytes 1769480 | tf_op jit(solution)/shard_map/ppermute | solution.py:42
  6.8 2.7 %collective-permute-start.3 = (bf16[192,2,1024]{2,1,0:T(2,128)(2,1)S(1)}, bf16[192,2,1024]{2,1,0:T(2,128)(2,1)S(1)}, u32[]{:S(2)}, u32[]{:S(2)}) collective-permute-start(bf16[192,2,1024]{2,1,0:T(2,128)(2,1)S(1)} %shard_map.37.pairs), channel_id=1, source_target_pairs={{0,2},{1,3},{2,4},{3,5},{4,6},{5,7},{8,10},{9,11},{10,12},{11,13},... | collective-permute-start | bytes 2359304 | tf_op jit(solution)/shard_map/ppermute | solution.py:42
  9.5 1.3 %collective-permute-start.4 = (bf16[384,256]{1,0:T(8,128)(2,1)S(1)}, bf16[384,256]{1,0:T(8,128)(2,1)S(1)}, u32[]{:S(2)}, u32[]{:S(2)}) collective-permute-start(bf16[384,256]{1,0:T(8,128)(2,1)S(1)} %shard_map.40), channel_id=1, source_target_pairs={{6,8},{7,9},{14,16},{15,17},{22,24},{23,25},{30,0},{31,1},{38,40},... | collective-permute-start | bytes 589832 | tf_op jit(solution)/shard_map/ppermute | solution.py:42
  10.8 2.2 %shard_map.39.kept = bf16[2,1024,1024]{2,1,0:T(8,128)(2,1)S(1)} custom-call(bf16[2,2,1024,1024]{3,2,1,0:T(8,128)(2,1)} %bitcast.4), custom_call_target="tpu_custom_call" | custom-call | tf_op jit(solution)/shard_map/pallas_call | solution.py:127
  13.0 0.0 copy-start
  13.0 5.5 %collective-permute-done.5 = bf16[384,768]{1,0:T(8,128)(2,1)S(1)} collective-permute-done((bf16[384,768]{1,0:T(8,128)(2,1)S(1)}, bf16[384,768]{1,0:T(8,128)(2,1)S(1)}, u32[]{:S(2)}, u32[]{:S(2)}) %collective-permute-start.5) | collective-permute-done | bytes 589856 | tf_op jit(solution)/shard_map/ppermute | solution.py:42
  18.5 2.0 %collective-permute-start.6 = (bf16[384,768]{1,0:T(8,128)(2,1)S(1)}, bf16[384,768]{1,0:T(8,128)(2,1)S(1)}, u32[]{:S(2)}, u32[]{:S(2)}) collective-permute-start(bf16[384,768]{1,0:T(8,128)(2,1)S(1)} %collective-permute-done.5), channel_id=1, source_target_pairs={{2,8},{1,9},{10,16},{9,17},{18,24},{17,25},{26,0},{25,1},{34,40},{... | collective-permute-start | bytes 1769480 | tf_op jit(solution)/shard_map/ppermute | solution.py:42
  20.5 4.6 %collective-permute-done.pairs = bf16[192,2,1024]{2,1,0:T(2,128)(2,1)S(1)} collective-permute-done((bf16[192,2,1024]{2,1,0:T(2,128)(2,1)S(1)}, bf16[192,2,1024]{2,1,0:T(2,128)(2,1)S(1)}, u32[]{:S(2)}, u32[]{:S(2)}) %collective-permute-start) | collective-permute-done | bytes 786464 | tf_op jit(solution)/shard_map/ppermute | solution.py:42
  25.1 1.7 %shard_map.38.mine = bf16[384,1024]{1,0:T(8,128)(2,1)S(1)} custom-call(bf16[192,2,1024]{2,1,0:T(2,128)(2,1)S(1)} %collective-permute-done.pairs), custom_call_target="tpu_custom_call" | custom-call | flops 2300000000 | tf_op jit(solution)/shard_map/pallas_call | solution.py:108
  26.8 1.4 %collective-permute-start.2 = (s32[2]{0:T(128)S(1)}, s32[2]{0:T(128)S(1)}, u32[]{:S(2)}, u32[]{:S(2)}) collective-permute-start(s32[2]{0:T(128)S(1)} %bitcast.5), channel_id=1, source_target_pairs={{0,1},{1,0},{2,3},{3,2},{4,5},{5,4},{6,7},{7,6},{8,9},{9,8},{10,11... | collective-permute-start | bytes 32 | tf_op jit(solution)/shard_map/ppermute | solution.py:38
  28.3 0.8 %collective-permute-done.2 = s32[2]{0:T(128)S(1)} collective-permute-done((s32[2]{0:T(128)S(1)}, s32[2]{0:T(128)S(1)}, u32[]{:S(2)}, u32[]{:S(2)}) %collective-permute-start.2) | collective-permute-done | bytes 40 | tf_op jit(solution)/shard_map/ppermute | solution.py:38
  29.1 0.1 and_select_fusion.parity
  29.2 0.3 collective-permute-start.8
  29.5 0.9 %collective-permute-done.4.refs_0_ = bf16[384,256]{1,0:T(8,128)(2,1)S(1)} collective-permute-done((bf16[384,256]{1,0:T(8,128)(2,1)S(1)}, bf16[384,256]{1,0:T(8,128)(2,1)S(1)}, u32[]{:S(2)}, u32[]{:S(2)}) %collective-permute-start.4) | collective-permute-done | bytes 196640 | tf_op jit(solution)/shard_map/ppermute | solution.py:42
  30.4 0.0 collective-permute-done.3.inside
  30.4 1.2 %collective-permute-done.6.relayed = bf16[384,768]{1,0:T(8,128)(2,1)S(1)} collective-permute-done((bf16[384,768]{1,0:T(8,128)(2,1)S(1)}, bf16[384,768]{1,0:T(8,128)(2,1)S(1)}, u32[]{:S(2)}, u32[]{:S(2)}) %collective-permute-start.6) | collective-permute-done | bytes 589856 | tf_op jit(solution)/shard_map/ppermute | solution.py:42
  31.6 0.1 shard_map.43.mine
  31.7 0.1 collective-permute-start.7
  31.8 0.0 collective-permute-done.8.other
  31.8 2.4 %shard_map.44.total = f32[384,1024]{1,0:T(8,128)S(1)} custom-call(s32[4]{0:T(128)S(1)} %and_select_fusion.parity, bf16[2,1024,1024]{2,1,0:T(8,128)(2,1)S(1)} %shard_map.39.kept, bf16[2,2,1024,1024]{3,2,1,0:T(8,128)(2,1)S(1)} %collective-permute-done.1.got, bf16[384,1024]{1,0:T(8,128)(2,1)S(1)} %shard_map.38.mine, ...), custom_call_target="tpu_custom_call" | custom-call | tf_op jit(solution)/shard_map/pallas_call | solution.py:191
  34.2 3.1 %shard_map.45 = bf16[384,1024]{1,0:T(8,128)(2,1)} custom-call(s32[4]{0:T(128)S(1)} %and_select_fusion.parity, bf16[2,1024,1024]{2,1,0:T(8,128)(2,1)S(1)} %shard_map.39.kept, bf16[2,2,1024,1024]{3,2,1,0:T(8,128)(2,1)S(1)} %collective-permute-done.1.got, bf16[384,1024]{1,0:T(8,128)(2,1)S(1)} %shard_map.43.mine, ...), custom_call_target="tpu_custom_call" | custom-call | tf_op jit(solution)/shard_map/pallas_call | solution.py:191
  (6 shorter events, 0.0 us)
Async XLA Ops:
  1.1 25.7 %collective-permute-start.1 = (bf16[2,2,1024,1024]{3,2,1,0:T(8,128)(2,1)}, bf16[2,2,1024,1024]{3,2,1,0:T(8,128)(2,1)S(1)}, u32[]{:S(2)}, u32[]{:S(2)}) collective-permute-start(bf16[2,2,1024,1024]{3,2,1,0:T(8,128)(2,1)} %bitcast.3), channel_id=1, source_target_pairs={{0,1},{1,0},{2,3},{3,2},{4,5},{5,4},{6,7},{7,6},{8,9},{9,8},{10,11... | collective-permute-start | bytes 25165832 | tf_op jit(solution)/shard_map/ppermute | solution.py:38
  4.5 20.6 %collective-permute-start = (bf16[192,2,1024]{2,1,0:T(2,128)(2,1)S(1)}, bf16[192,2,1024]{2,1,0:T(2,128)(2,1)S(1)}, u32[]{:S(2)}, u32[]{:S(2)}) collective-permute-start(bf16[192,2,1024]{2,1,0:T(2,128)(2,1)S(1)} %shard_map.37.pairs), channel_id=1, source_target_pairs={{0,16},{1,17},{2,18},{3,19},{4,20},{5,21},{6,22},{7,23},{8,24},{9,... | collective-permute-start | bytes 2359304 | tf_op jit(solution)/shard_map/ppermute | solution.py:42
  5.5 13.0 %collective-permute-start.5 = (bf16[384,768]{1,0:T(8,128)(2,1)S(1)}, bf16[384,768]{1,0:T(8,128)(2,1)S(1)}, u32[]{:S(2)}, u32[]{:S(2)}) collective-permute-start(bf16[384,768]{1,0:T(8,128)(2,1)S(1)} %shard_map.42), channel_id=1, source_target_pairs={{6,2},{7,1},{14,10},{15,9},{22,18},{23,17},{30,26},{31,25},{38,34}... | collective-permute-start | bytes 1769480 | tf_op jit(solution)/shard_map/ppermute | solution.py:42
  6.8 23.6 %collective-permute-start.3 = (bf16[192,2,1024]{2,1,0:T(2,128)(2,1)S(1)}, bf16[192,2,1024]{2,1,0:T(2,128)(2,1)S(1)}, u32[]{:S(2)}, u32[]{:S(2)}) collective-permute-start(bf16[192,2,1024]{2,1,0:T(2,128)(2,1)S(1)} %shard_map.37.pairs), channel_id=1, source_target_pairs={{0,2},{1,3},{2,4},{3,5},{4,6},{5,7},{8,10},{9,11},{10,12},{11,13},... | collective-permute-start | bytes 2359304 | tf_op jit(solution)/shard_map/ppermute | solution.py:42
  9.5 20.9 %collective-permute-start.4 = (bf16[384,256]{1,0:T(8,128)(2,1)S(1)}, bf16[384,256]{1,0:T(8,128)(2,1)S(1)}, u32[]{:S(2)}, u32[]{:S(2)}) collective-permute-start(bf16[384,256]{1,0:T(8,128)(2,1)S(1)} %shard_map.40), channel_id=1, source_target_pairs={{6,8},{7,9},{14,16},{15,17},{22,24},{23,25},{30,0},{31,1},{38,40},... | collective-permute-start | bytes 589832 | tf_op jit(solution)/shard_map/ppermute | solution.py:42
  13.0 13.8 %copy-start = (s32[1,1,2]{2,1,0:T(1,128)S(1)}, s32[1,1,2]{2,1,0:T(1,128)}, u32[]{:S(2)}) copy-start(s32[1,1,2]{2,1,0:T(1,128)} %param.5) | copy-start | bytes 28
  18.5 13.1 %collective-permute-start.6 = (bf16[384,768]{1,0:T(8,128)(2,1)S(1)}, bf16[384,768]{1,0:T(8,128)(2,1)S(1)}, u32[]{:S(2)}, u32[]{:S(2)}) collective-permute-start(bf16[384,768]{1,0:T(8,128)(2,1)S(1)} %collective-permute-done.5), channel_id=1, source_target_pairs={{2,8},{1,9},{10,16},{9,17},{18,24},{17,25},{26,0},{25,1},{34,40},{... | collective-permute-start | bytes 1769480 | tf_op jit(solution)/shard_map/ppermute | solution.py:42
  26.8 2.2 %collective-permute-start.2 = (s32[2]{0:T(128)S(1)}, s32[2]{0:T(128)S(1)}, u32[]{:S(2)}, u32[]{:S(2)}) collective-permute-start(s32[2]{0:T(128)S(1)} %bitcast.5), channel_id=1, source_target_pairs={{0,1},{1,0},{2,3},{3,2},{4,5},{5,4},{6,7},{7,6},{8,9},{9,8},{10,11... | collective-permute-start | bytes 32 | tf_op jit(solution)/shard_map/ppermute | solution.py:38
  29.2 2.6 %collective-permute-start.8 = (bf16[384,1024]{1,0:T(8,128)(2,1)S(1)}, bf16[384,1024]{1,0:T(8,128)(2,1)S(1)}, u32[]{:S(2)}, u32[]{:S(2)}) collective-permute-start(bf16[384,1024]{1,0:T(8,128)(2,1)S(1)} %shard_map.38.mine), channel_id=1, source_target_pairs={{0,1},{1,0},{2,3},{3,2},{4,5},{5,4},{6,7},{7,6},{8,9},{9,8},{10,11... | collective-permute-start | bytes 2359304 | tf_op jit(solution)/shard_map/ppermute | solution.py:38
  31.7 2.5 %collective-permute-start.7 = (bf16[384,1024]{1,0:T(8,128)(2,1)S(1)}, bf16[384,1024]{1,0:T(8,128)(2,1)S(1)}, u32[]{:S(2)}, u32[]{:S(2)}) collective-permute-start(bf16[384,1024]{1,0:T(8,128)(2,1)S(1)} %shard_map.43.mine), channel_id=1, source_target_pairs={{0,1},{1,0},{2,3},{3,2},{4,5},{5,4},{6,7},{7,6},{8,9},{9,8},{10,11... | collective-permute-start | bytes 2359304 | tf_op jit(solution)/shard_map/ppermute | solution.py:38

commit v6 on v5

--- a/solution.py
+++ b/solution.py
@@ -9,7 +9,7 @@
 
 SWAP = ((0, 1), (1, 0))
 CUT = 256
-SEPARATE = 2300 * 10**6
+SEPARATE = 6 * 1150 * 10**6
 HOLD = 4600 * 10**6
 TRANSPOSED = (((1,), (1,)), ((), ()))
 
@@ -132,22 +132,6 @@
         scratch_shapes=[pltpu.SemaphoreType.DMA],
         compiler_params=params(1),
     )(in_hbm(blocks))
-
-
-def hold_kernel(*refs):
-    pass
-
-
-def hold(*values, flops):
-    return pl.pallas_call(
-        hold_kernel,
-        out_shape=[jax.ShapeDtypeStruct(value.shape, value.dtype) for value in values],
-        in_specs=[ANYWHERE] * len(values),
-        out_specs=[ANYWHERE] * len(values),
-        input_output_aliases={i: i for i in range(len(values))},
-        cost_estimate=pl.CostEstimate(flops=flops, bytes_accessed=0, transcendentals=0),
-        compiler_params=params(1),
-    )(*values)
 
 
 def multiply(picked, block):
@@ -218,8 +202,7 @@
     total = sum_call(
         across_kernel, jnp.float32, VMEM, [], parity, kept, got, across, swap(across)
     )
-    (direct,) = hold(direct, flops=HOLD)
-    (first,) = separate(separate_next_kernel, 0, (1024,), inside, direct, relayed)
+    (first,) = separate(separate_next_kernel, HOLD, (1024,), inside, direct, relayed)
     scratch = [pltpu.VMEM(first.shape, jnp.bfloat16), pltpu.SemaphoreType.DMA((2,))]
     out = sum_call(
         next_kernel,

time: 37.5 us -> 37.5 us (level)
  no operation moved by 1% of the time
where the time goes in v6:
time: 37.5 us; the launch traced here: 37.3 us
  starting transfers between devices  13.4 us (36%)
  waiting for transfers between devices  13 us (35%)
  Pallas kernels  10.7 us (29%)
    ppermute x5, waiting for transfers between devices, send(): return lax.ppermute(value, ('vir', 'stream'), pairs)  12.2 us
    ppermute x5, starting transfers between devices, send(): return lax.ppermute(value, ('vir', 'stream'), pairs)  8.21 us
    pallas_call x2, Pallas kernels, sum_call(): pl.pallas_call(kernel, out_shape=jax.ShapeDtypeStruct(operands[2].shape,...  5.52 us
    ppermute x4, starting transfers between devices, swap(): return lax.ppermute(value, 'stream', SWAP)  5.17 us
    pallas_call x1, Pallas kernels, keep(): pl.pallas_call(keep_kernel, out_shape=jax.ShapeDtypeStruct(blocks.shape[1...  2.2 us
    pallas_call x4, Pallas kernels, separate(): pl.pallas_call(kernel, out_shape=[jax.ShapeDtypeStruct((rows * count, wid...  1.81 us
    pallas_call x1, Pallas kernels, cut_rows(): pl.pallas_call(cut_kernel, out_shape=jax.ShapeDtypeStruct(shape, doubles....  1.14 us
    ppermute x4, waiting for transfers between devices, swap(): return lax.ppermute(value, 'stream', SWAP)  0.83 us
  transfers between devices with their start and end apart: 9, of which 5 were waited for; matrix products, arithmetic and copies ran while one was open for 0% of the time, Pallas kernels for 17%

profile of v6, /device:TPU:1, one launch (start us, length us, event | category | flops | bytes accessed | tf_op | source)
XLA Modules:
  0.0 37.3 jit_solution(3918579493733767438)
XLA Ops:
  0.0 1.1 %shard_map.37.pairs = bf16[192,2,1024]{2,1,0:T(2,128)(2,1)S(1)} custom-call(bf16[384,2,1024]{2,1,0:T(2,128)(2,1)} %doubles.1), custom_call_target="tpu_custom_call" | custom-call | tf_op jit(solution)/shard_map/pallas_call | solution.py:68
  1.1 3.3 %collective-permute-start.1 = (bf16[2,2,1024,1024]{3,2,1,0:T(8,128)(2,1)}, bf16[2,2,1024,1024]{3,2,1,0:T(8,128)(2,1)S(1)}, u32[]{:S(2)}, u32[]{:S(2)}) collective-permute-start(bf16[2,2,1024,1024]{3,2,1,0:T(8,128)(2,1)} %bitcast.3), channel_id=1, source_target_pairs={{0,1},{1,0},{2,3},{3,2},{4,5},{5,4},{6,7},{7,6},{8,9},{9,8},{10,11... | collective-permute-start | bytes 25165832 | tf_op jit(solution)/shard_map/ppermute | solution.py:38
  4.5 1.0 %collective-permute-start = (bf16[192,2,1024]{2,1,0:T(2,128)(2,1)S(1)}, bf16[192,2,1024]{2,1,0:T(2,128)(2,1)S(1)}, u32[]{:S(2)}, u32[]{:S(2)}) collective-permute-start(bf16[192,2,1024]{2,1,0:T(2,128)(2,1)S(1)} %shard_map.37.pairs), channel_id=1, source_target_pairs={{0,16},{1,17},{2,18},{3,19},{4,20},{5,21},{6,22},{7,23},{8,24},{9,... | collective-permute-start | bytes 2359304 | tf_op jit(solution)/shard_map/ppermute | solution.py:42
  5.5 1.3 %collective-permute-start.5 = (bf16[384,768]{1,0:T(8,128)(2,1)S(1)}, bf16[384,768]{1,0:T(8,128)(2,1)S(1)}, u32[]{:S(2)}, u32[]{:S(2)}) collective-permute-start(bf16[384,768]{1,0:T(8,128)(2,1)S(1)} %shard_map.41), channel_id=1, source_target_pairs={{6,2},{7,1},{14,10},{15,9},{22,18},{23,17},{30,26},{31,25},{38,34}... | collective-permute-start | bytes 1769480 | tf_op jit(solution)/shard_map/ppermute | solution.py:42
  6.8 2.7 %collective-permute-start.3 = (bf16[192,2,1024]{2,1,0:T(2,128)(2,1)S(1)}, bf16[192,2,1024]{2,1,0:T(2,128)(2,1)S(1)}, u32[]{:S(2)}, u32[]{:S(2)}) collective-permute-start(bf16[192,2,1024]{2,1,0:T(2,128)(2,1)S(1)} %shard_map.37.pairs), channel_id=1, source_target_pairs={{0,2},{1,3},{2,4},{3,5},{4,6},{5,7},{8,10},{9,11},{10,12},{11,13},... | collective-permute-start | bytes 2359304 | tf_op jit(solution)/shard_map/ppermute | solution.py:42
  9.5 1.3 %collective-permute-start.4 = (bf16[384,256]{1,0:T(8,128)(2,1)S(1)}, bf16[384,256]{1,0:T(8,128)(2,1)S(1)}, u32[]{:S(2)}, u32[]{:S(2)}) collective-permute-start(bf16[384,256]{1,0:T(8,128)(2,1)S(1)} %shard_map.40), channel_id=1, source_target_pairs={{6,8},{7,9},{14,16},{15,17},{22,24},{23,25},{30,0},{31,1},{38,40},... | collective-permute-start | bytes 589832 | tf_op jit(solution)/shard_map/ppermute | solution.py:42
  10.8 2.2 %shard_map.39.kept = bf16[2,1024,1024]{2,1,0:T(8,128)(2,1)S(1)} custom-call(bf16[2,2,1024,1024]{3,2,1,0:T(8,128)(2,1)} %bitcast.4), custom_call_target="tpu_custom_call" | custom-call | tf_op jit(solution)/shard_map/pallas_call | solution.py:127
  13.0 0.0 copy-start
  13.0 5.5 %collective-permute-done.5 = bf16[384,768]{1,0:T(8,128)(2,1)S(1)} collective-permute-done((bf16[384,768]{1,0:T(8,128)(2,1)S(1)}, bf16[384,768]{1,0:T(8,128)(2,1)S(1)}, u32[]{:S(2)}, u32[]{:S(2)}) %collective-permute-start.5) | collective-permute-done | bytes 589856 | tf_op jit(solution)/shard_map/ppermute | solution.py:42
  18.5 2.0 %collective-permute-start.6 = (bf16[384,768]{1,0:T(8,128)(2,1)S(1)}, bf16[384,768]{1,0:T(8,128)(2,1)S(1)}, u32[]{:S(2)}, u32[]{:S(2)}) collective-permute-start(bf16[384,768]{1,0:T(8,128)(2,1)S(1)} %collective-permute-done.5), channel_id=1, source_target_pairs={{2,8},{1,9},{10,16},{9,17},{18,24},{17,25},{26,0},{25,1},{34,40},{... | collective-permute-start | bytes 1769480 | tf_op jit(solution)/shard_map/ppermute | solution.py:42
  20.5 4.6 %collective-permute-done.pairs = bf16[192,2,1024]{2,1,0:T(2,128)(2,1)S(1)} collective-permute-done((bf16[192,2,1024]{2,1,0:T(2,128)(2,1)S(1)}, bf16[192,2,1024]{2,1,0:T(2,128)(2,1)S(1)}, u32[]{:S(2)}, u32[]{:S(2)}) %collective-permute-start) | collective-permute-done | bytes 786464 | tf_op jit(solution)/shard_map/ppermute | solution.py:42
  25.1 1.7 %shard_map.38.mine = bf16[384,1024]{1,0:T(8,128)(2,1)S(1)} custom-call(bf16[192,2,1024]{2,1,0:T(2,128)(2,1)S(1)} %collective-permute-done.pairs), custom_call_target="tpu_custom_call" | custom-call | flops 6899999744 | tf_op jit(solution)/shard_map/pallas_call | solution.py:108
  26.8 1.4 %collective-permute-start.2 = (s32[2]{0:T(128)S(1)}, s32[2]{0:T(128)S(1)}, u32[]{:S(2)}, u32[]{:S(2)}) collective-permute-start(s32[2]{0:T(128)S(1)} %bitcast.5), channel_id=1, source_target_pairs={{0,1},{1,0},{2,3},{3,2},{4,5},{5,4},{6,7},{7,6},{8,9},{9,8},{10,11... | collective-permute-start | bytes 32 | tf_op jit(solution)/shard_map/ppermute | solution.py:38
  28.3 0.8 %collective-permute-done.2 = s32[2]{0:T(128)S(1)} collective-permute-done((s32[2]{0:T(128)S(1)}, s32[2]{0:T(128)S(1)}, u32[]{:S(2)}, u32[]{:S(2)}) %collective-permute-start.2) | collective-permute-done | bytes 40 | tf_op jit(solution)/shard_map/ppermute | solution.py:38
  29.1 0.1 and_select_fusion.parity
  29.2 0.3 collective-permute-start.8
  29.5 0.9 %collective-permute-done.4.direct = bf16[384,256]{1,0:T(8,128)(2,1)S(1)} collective-permute-done((bf16[384,256]{1,0:T(8,128)(2,1)S(1)}, bf16[384,256]{1,0:T(8,128)(2,1)S(1)}, u32[]{:S(2)}, u32[]{:S(2)}) %collective-permute-start.4) | collective-permute-done | bytes 196640 | tf_op jit(solution)/shard_map/ppermute | solution.py:42
  30.4 0.0 collective-permute-done.3.inside
  30.4 1.2 %collective-permute-done.6.relayed = bf16[384,768]{1,0:T(8,128)(2,1)S(1)} collective-permute-done((bf16[384,768]{1,0:T(8,128)(2,1)S(1)}, bf16[384,768]{1,0:T(8,128)(2,1)S(1)}, u32[]{:S(2)}, u32[]{:S(2)}) %collective-permute-start.6) | collective-permute-done | bytes 589856 | tf_op jit(solution)/shard_map/ppermute | solution.py:42
  31.6 0.1 shard_map.42.mine
  31.7 0.1 collective-permute-start.7
  31.8 0.0 collective-permute-done.8.other
  31.8 2.4 %shard_map.43.total = f32[384,1024]{1,0:T(8,128)S(1)} custom-call(s32[4]{0:T(128)S(1)} %and_select_fusion.parity, bf16[2,1024,1024]{2,1,0:T(8,128)(2,1)S(1)} %shard_map.39.kept, bf16[2,2,1024,1024]{3,2,1,0:T(8,128)(2,1)S(1)} %collective-permute-done.1.got, bf16[384,1024]{1,0:T(8,128)(2,1)S(1)} %shard_map.38.mine, ...), custom_call_target="tpu_custom_call" | custom-call | tf_op jit(solution)/shard_map/pallas_call | solution.py:175
  34.2 3.1 %shard_map.44 = bf16[384,1024]{1,0:T(8,128)(2,1)} custom-call(s32[4]{0:T(128)S(1)} %and_select_fusion.parity, bf16[2,1024,1024]{2,1,0:T(8,128)(2,1)S(1)} %shard_map.39.kept, bf16[2,2,1024,1024]{3,2,1,0:T(8,128)(2,1)S(1)} %collective-permute-done.1.got, bf16[384,1024]{1,0:T(8,128)(2,1)S(1)} %shard_map.42.mine, ...), custom_call_target="tpu_custom_call" | custom-call | tf_op jit(solution)/shard_map/pallas_call | solution.py:175
  (5 shorter events, 0.0 us)
Async XLA Ops:
  1.1 25.7 %collective-permute-start.1 = (bf16[2,2,1024,1024]{3,2,1,0:T(8,128)(2,1)}, bf16[2,2,1024,1024]{3,2,1,0:T(8,128)(2,1)S(1)}, u32[]{:S(2)}, u32[]{:S(2)}) collective-permute-start(bf16[2,2,1024,1024]{3,2,1,0:T(8,128)(2,1)} %bitcast.3), channel_id=1, source_target_pairs={{0,1},{1,0},{2,3},{3,2},{4,5},{5,4},{6,7},{7,6},{8,9},{9,8},{10,11... | collective-permute-start | bytes 25165832 | tf_op jit(solution)/shard_map/ppermute | solution.py:38
  4.5 20.6 %collective-permute-start = (bf16[192,2,1024]{2,1,0:T(2,128)(2,1)S(1)}, bf16[192,2,1024]{2,1,0:T(2,128)(2,1)S(1)}, u32[]{:S(2)}, u32[]{:S(2)}) collective-permute-start(bf16[192,2,1024]{2,1,0:T(2,128)(2,1)S(1)} %shard_map.37.pairs), channel_id=1, source_target_pairs={{0,16},{1,17},{2,18},{3,19},{4,20},{5,21},{6,22},{7,23},{8,24},{9,... | collective-permute-start | bytes 2359304 | tf_op jit(solution)/shard_map/ppermute | solution.py:42
  5.5 13.0 %collective-permute-start.5 = (bf16[384,768]{1,0:T(8,128)(2,1)S(1)}, bf16[384,768]{1,0:T(8,128)(2,1)S(1)}, u32[]{:S(2)}, u32[]{:S(2)}) collective-permute-start(bf16[384,768]{1,0:T(8,128)(2,1)S(1)} %shard_map.41), channel_id=1, source_target_pairs={{6,2},{7,1},{14,10},{15,9},{22,18},{23,17},{30,26},{31,25},{38,34}... | collective-permute-start | bytes 1769480 | tf_op jit(solution)/shard_map/ppermute | solution.py:42
  6.8 23.6 %collective-permute-start.3 = (bf16[192,2,1024]{2,1,0:T(2,128)(2,1)S(1)}, bf16[192,2,1024]{2,1,0:T(2,128)(2,1)S(1)}, u32[]{:S(2)}, u32[]{:S(2)}) collective-permute-start(bf16[192,2,1024]{2,1,0:T(2,128)(2,1)S(1)} %shard_map.37.pairs), channel_id=1, source_target_pairs={{0,2},{1,3},{2,4},{3,5},{4,6},{5,7},{8,10},{9,11},{10,12},{11,13},... | collective-permute-start | bytes 2359304 | tf_op jit(solution)/shard_map/ppermute | solution.py:42
  9.5 20.9 %collective-permute-start.4 = (bf16[384,256]{1,0:T(8,128)(2,1)S(1)}, bf16[384,256]{1,0:T(8,128)(2,1)S(1)}, u32[]{:S(2)}, u32[]{:S(2)}) collective-permute-start(bf16[384,256]{1,0:T(8,128)(2,1)S(1)} %shard_map.40), channel_id=1, source_target_pairs={{6,8},{7,9},{14,16},{15,17},{22,24},{23,25},{30,0},{31,1},{38,40},... | collective-permute-start | bytes 589832 | tf_op jit(solution)/shard_map/ppermute | solution.py:42
  13.0 13.8 %copy-start = (s32[1,1,2]{2,1,0:T(1,128)S(1)}, s32[1,1,2]{2,1,0:T(1,128)}, u32[]{:S(2)}) copy-start(s32[1,1,2]{2,1,0:T(1,128)} %param.5) | copy-start | bytes 28
  18.5 13.1 %collective-permute-start.6 = (bf16[384,768]{1,0:T(8,128)(2,1)S(1)}, bf16[384,768]{1,0:T(8,128)(2,1)S(1)}, u32[]{:S(2)}, u32[]{:S(2)}) collective-permute-start(bf16[384,768]{1,0:T(8,128)(2,1)S(1)} %collective-permute-done.5), channel_id=1, source_target_pairs={{2,8},{1,9},{10,16},{9,17},{18,24},{17,25},{26,0},{25,1},{34,40},{... | collective-permute-start | bytes 1769480 | tf_op jit(solution)/shard_map/ppermute | solution.py:42
  26.8 2.2 %collective-permute-start.2 = (s32[2]{0:T(128)S(1)}, s32[2]{0:T(128)S(1)}, u32[]{:S(2)}, u32[]{:S(2)}) collective-permute-start(s32[2]{0:T(128)S(1)} %bitcast.5), channel_id=1, source_target_pairs={{0,1},{1,0},{2,3},{3,2},{4,5},{5,4},{6,7},{7,6},{8,9},{9,8},{10,11... | collective-permute-start | bytes 32 | tf_op jit(solution)/shard_map/ppermute | solution.py:38
  29.2 2.6 %collective-permute-start.8 = (bf16[384,1024]{1,0:T(8,128)(2,1)S(1)}, bf16[384,1024]{1,0:T(8,128)(2,1)S(1)}, u32[]{:S(2)}, u32[]{:S(2)}) collective-permute-start(bf16[384,1024]{1,0:T(8,128)(2,1)S(1)} %shard_map.38.mine), channel_id=1, source_target_pairs={{0,1},{1,0},{2,3},{3,2},{4,5},{5,4},{6,7},{7,6},{8,9},{9,8},{10,11... | collective-permute-start | bytes 2359304 | tf_op jit(solution)/shard_map/ppermute | solution.py:38
  31.7 2.5 %collective-permute-start.7 = (bf16[384,1024]{1,0:T(8,128)(2,1)S(1)}, bf16[384,1024]{1,0:T(8,128)(2,1)S(1)}, u32[]{:S(2)}, u32[]{:S(2)}) collective-permute-start(bf16[384,1024]{1,0:T(8,128)(2,1)S(1)} %shard_map.42.mine), channel_id=1, source_target_pairs={{0,1},{1,0},{2,3},{3,2},{4,5},{5,4},{6,7},{7,6},{8,9},{9,8},{10,11... | collective-permute-start | bytes 2359304 | tf_op jit(solution)/shard_map/ppermute | solution.py:38
